TPU v7x, 32 devices: a whole 2x2x4 slice. The times are simulated.
32 devices in a mesh: seq: 4 (over y, x), head: 8 (over z, core).
Axes of the slice: x: 2, y: 2, z: 4, core: 2. Of those that a mesh axis runs over, the one named last changes fastest.
Arguments:
- query_rows: bfloat16 [8192, 64, 128], P('seq', 'head'), may hold values from -112 to 112
- key_rows: bfloat16 [8192, 64, 128], P('seq', 'head'), may hold values from -4 to 4
- value_rows: bfloat16 [8192, 64, 128], P('seq', 'head'), may hold values from -6 to 6
- attn_output: bfloat16 [8192, 64, 128], P('seq', 'head'), may hold values from -6 to 6
- out_grad: bfloat16 [8192, 4, 2048], P(('seq', 'head')), may hold values from -6 to 6
- neighbours: int32 [64, 4], replicated, may hold values from 0 to 63, as said below
- counts: int32 [64], replicated, may hold values from 2 to 128
Outputs:
- grad_query: bfloat16 [8192, 4, 2048], P(('seq', 'head'))
- grad_key: bfloat16 [8192, 4, 2048], P(('seq', 'head'))
- grad_value: bfloat16 [8192, 4, 2048], P(('seq', 'head'))
Inputs may be any that keep to these rules, and one draw needn't show every extreme that they name: `neighbours`: row t lists 4 different tiles, the first being t itself, each at most half of 16 tiles away from t.
All inputs are finite; a program needn't handle non-finite values.
Results may differ from a plain program's by a relative error of at most 0.011.
Values may be sent and summed in bfloat16 or wider, within the bound.
A program may use at most 256 MiB of HBM per device.

v0:
```python
import jax
import jax.numpy as jnp
from jax import lax
from jax.sharding import PartitionSpec as P

TILE = 128


def with_halo(block, sides, width):
    for axis, dim in sides:
        count = lax.axis_size(axis)
        forward = [(i, i + 1) for i in range(count - 1)]
        backward = [(target, source) for source, target in forward]
        low = lax.ppermute(
            lax.slice_in_dim(block, block.shape[dim] - width, None, axis=dim), axis, forward
        )
        high = lax.ppermute(lax.slice_in_dim(block, 0, width, axis=dim), axis, backward)
        block = jnp.concatenate([low, block, high], axis=dim)
    return block


def pair_block(query, grad_rows, delta_rows, lists, kv_tiles, key_valid, scale_factor, log_rows):
    head_dim = query.shape[-1]
    gathered = kv_tiles[lists]
    key_near = gathered[..., :head_dim]
    value_near = gathered[..., head_dim:]
    valid_near = key_valid[lists]
    scores = (
        jnp.einsum("icgd,injgd->icgnj", query, key_near, preferred_element_type=jnp.float32)
        * scale_factor
    )
    scores = jnp.where(valid_near[:, None, None, :, :], scores, -jnp.inf)
    row_max = jnp.max(scores, axis=(3, 4))
    log_rows = row_max + jnp.log(jnp.sum(jnp.exp(scores - row_max[..., None, None]), axis=(3, 4)))
    attn_probs = jnp.exp(scores - log_rows[..., None, None])
    dprobs = jnp.einsum(
        "icgd,injgd->icgnj", grad_rows, value_near, preferred_element_type=jnp.float32
    )
    dscore = (attn_probs * (dprobs - delta_rows[..., None, None]) * scale_factor).astype(
        jnp.bfloat16
    )
    probs_low = attn_probs.astype(jnp.bfloat16)
    dquery = jnp.einsum("icgnj,injgd->icgd", dscore, key_near, preferred_element_type=jnp.float32)
    dkey_terms = jnp.einsum("icgnj,icgd->injgd", dscore, query, preferred_element_type=jnp.float32)
    dvalue_terms = jnp.einsum(
        "icgnj,icgd->injgd", probs_low, grad_rows, preferred_element_type=jnp.float32
    )
    return (dquery, log_rows, jnp.concatenate([dkey_terms, dvalue_terms], axis=-1))


def per_device(query_rows, key_rows, value_rows, attn_output, out_grad, neighbours, counts):
    seq_rows, batch, width = out_grad.shape
    shard_tokens, group, head_dim = query_rows.shape
    tile_len = TILE
    nbr_count = neighbours.shape[1]
    tiles_all = counts.shape[0]
    tiles_dev = shard_tokens // tile_len
    half_tiles = tiles_dev // 2
    half_tokens = shard_tokens // 2
    scale_factor = head_dim ** (-0.5)
    block_tiles = min(4, tiles_dev)
    block_count = tiles_dev // block_tiles
    grads_in = lax.all_to_all(
        out_grad.reshape(seq_rows, batch * width // head_dim, head_dim),
        "head",
        split_axis=1,
        concat_axis=0,
        tiled=True,
    )
    shard_index = lax.axis_index("seq")
    first_tile = shard_index * tiles_dev
    ext_base = first_tile - half_tiles
    ext_tiles = ext_base + jnp.arange(2 * tiles_dev, dtype=jnp.int32)
    tile_table = jnp.arange(tiles_all, dtype=jnp.int32)
    ext_counts = jnp.sum(
        jnp.where(ext_tiles[:, None] == tile_table[None, :], counts[None, :], 0), axis=1
    )
    positions = jnp.arange(tile_len, dtype=jnp.int32)
    key_valid = positions[None, :] < ext_counts[:, None]
    own_counts = lax.dynamic_slice_in_dim(counts, first_tile, tiles_dev, 0)
    own_valid = (positions[None, :] < own_counts[:, None]).reshape(shard_tokens)
    grad_rows = grads_in * own_valid[:, None, None].astype(jnp.bfloat16)
    delta = jnp.einsum("tgd,tgd->tg", grad_rows, attn_output, preferred_element_type=jnp.float32)
    kv_pairs = jnp.concatenate([key_rows, value_rows], axis=2)
    kv_ext = with_halo(kv_pairs, (("seq", 0),), half_tokens)
    kv_tiles = kv_ext.reshape(2 * tiles_dev, tile_len, group, 2 * head_dim)
    own_lists = lax.dynamic_slice_in_dim(neighbours, first_tile, tiles_dev, 0) - ext_base

    def own_step(totals, inputs):
        query_blk, grad_blk, delta_blk, list_blk = inputs
        dquery, log_blk, dkv_terms = pair_block(
            query_blk, grad_blk, delta_blk, list_blk, kv_tiles, key_valid, scale_factor, None
        )
        totals = totals.at[list_blk.reshape(-1)].add(
            dkv_terms.reshape(-1, tile_len, group, 2 * head_dim)
        )
        return (totals, (dquery, log_blk))

    inputs_own = (
        query_rows.reshape(block_count, block_tiles, tile_len, group, head_dim),
        grad_rows.reshape(block_count, block_tiles, tile_len, group, head_dim),
        delta.reshape(block_count, block_tiles, tile_len, group),
        own_lists.reshape(block_count, block_tiles, nbr_count),
    )
    start_totals = jnp.zeros((2 * tiles_dev, tile_len, group, 2 * head_dim), jnp.float32)
    totals, (dquery_all, log_all) = lax.scan(own_step, start_totals, inputs_own)
    grad_q = dquery_all.reshape(shard_tokens, group, head_dim).astype(jnp.bfloat16)
    totals = totals.reshape(2 * shard_tokens, group, 2 * head_dim)
    middle = totals[half_tokens : half_tokens + shard_tokens]
    flanks = jnp.concatenate([totals[:half_tokens], totals[half_tokens + shard_tokens :]], axis=0)
    returned = with_halo(flanks.astype(jnp.bfloat16), (("seq", 0),), half_tokens).astype(
        flanks.dtype
    )
    own_grads = middle + jnp.concatenate(
        [returned[:half_tokens], returned[half_tokens + shard_tokens :]], axis=0
    )
    grad_k = own_grads[..., :head_dim].astype(jnp.bfloat16)
    grad_v = own_grads[..., head_dim:].astype(jnp.bfloat16)
    back_q, back_k, back_v = (
        lax.all_to_all(grad_q, "head", split_axis=0, concat_axis=1, tiled=True),
        lax.all_to_all(grad_k, "head", split_axis=0, concat_axis=1, tiled=True),
        lax.all_to_all(grad_v, "head", split_axis=0, concat_axis=1, tiled=True),
    )
    return (
        back_q.reshape(seq_rows, batch, width),
        back_k.reshape(seq_rows, batch, width),
        back_v.reshape(seq_rows, batch, width),
    )


def solution(mesh):
    placed = (
        P("seq", "head", None),
        P("seq", "head", None),
        P("seq", "head", None),
        P("seq", "head", None),
        P(("seq", "head"), None, None),
        P(),
        P(),
    )
    return jax.shard_map(
        per_device,
        mesh=mesh,
        in_specs=placed,
        out_specs=(
            P(("seq", "head"), None, None),
            P(("seq", "head"), None, None),
            P(("seq", "head"), None, None),
        ),
        check_vma=False,
    )
```

profile of v0, /device:TPU:4, one launch (start us, length us, event | category | flops | bytes accessed | tf_op | source)
XLA Modules:
  0.0 1140.1 jit_solution(3865516001835990160)
XLA Ops:
  37.1 89.0 %collective-permute-done = bf16[1024,8,256]{2,1,0:T(8,128)(2,1)} collective-permute-done((bf16[1024,8,256]{2,1,0:T(8,128)(2,1)}, bf16[1024,8,256]{2,1,0:T(8,128)(2,1)}, u32[]{:S(2)}, u32[]{:S(2)}) %collective-permute-start) | collective-permute-done | bytes 4194336 | tf_op jit(solution)/shard_map/ppermute | solution.py:14
  126.2 87.6 %collective-permute-done.1 = bf16[1024,8,256]{2,1,0:T(8,128)(2,1)} collective-permute-done((bf16[1024,8,256]{2,1,0:T(8,128)(2,1)}, bf16[1024,8,256]{2,1,0:T(8,128)(2,1)}, u32[]{:S(2)}, u32[]{:S(2)}) %collective-permute-start.1) | collective-permute-done | bytes 4194336 | tf_op jit(solution)/shard_map/ppermute | solution.py:17
  213.8 18.3 %pad_maximum_fusion.1 = bf16[4096,8,256]{2,1,0:T(8,128)(2,1)} fusion(bf16[1024,8,256]{2,1,0:T(8,128)(2,1)} %collective-permute-done.1, bf16[2048,8,256]{2,1,0:T(8,128)(2,1)} %copy-done.2, bf16[1024,8,256]{2,1,0:T(8,128)(2,1)} %collective-permute-done), kind=kLoop, calls=%fused_computation.46 | loop fusion | flops 16777216 | bytes 33554432 | tf_op jit(solution)/shard_map/concatenate | solution.py:18
  239.1 28.9 %fusion.33 = f32[2048,8]{1,0:T(8,128)S(1)} fusion(bf16[2048,8,128]{2,1,0:T(8,128)(2,1)S(1)} %copy-done.5, bf16[2048,8,128]{2,1,0:T(8,128)(2,1)S(1)} %bitcast.151, bf16[2048]{0:T(1024)(128)(2,1)S(1)} %fusion.37), kind=kLoop, calls=%fused_computation.50 | loop fusion | flops 10469376 | bytes 8458240
  274.1 11.1 broadcast_in_dim.31
  285.2 390.4 %while.13 = (s32[]{:T(128)}, f32[32,128,8,256]{3,2,1,0:T(8,128)}, bf16[4,4,128,8,128]{4,3,2,1,0:T(8,128)(2,1)}, s32[4,4,4]{2,1,0:T(4,128)S(1)}, bf16[4,4,128,8,1...) while((s32[]{:T(128)}, f32[32,128,8,256]{3,2,1,0:T(8,128)}, ...), condition=%wide.region_5.6_spmd.clone, body=%wide.region_1.5_spmd.clone.sunk | while | flops 2730492928 | bytes 282268800 | solution.py:106
  287.7 10.6 gather_fusion.1
  328.4 19.9 %copy.185 = f32[4,4,128,8,256]{4,3,2,1,0:T(8,128)} copy(f32[4,4,128,8,256]{2,4,1,3,0:T(8,128)} %pad_maximum_fusion.6) | data formatting | bytes 33554432 | tf_op jit(solution)/shard_map/while/body/eval_jaxpr/concatenate | solution.py:48
  348.3 34.4 %scatter_fusion = f32[32,128,8,256]{3,2,1,0:T(8,128)} fusion(f32[32,128,8,256]{3,2,1,0:T(8,128)} %get-tuple-element.256, s32[16]{0:T(128)S(1)} %fusion.60, f32[16,128,8,256]{3,2,1,0:T(8,128)} %bitcast.144), kind=kCustom, calls=%fused_computation.2.clone.clone.1 | custom fusion | flops 4194304 | bytes 50331712 | tf_op jit(solution)/shard_map/while/body/eval_jaxpr/scatter-add | solution.py:94
  385.3 10.6 gather_fusion.1
  426.1 19.9 %copy.185 = f32[4,4,128,8,256]{4,3,2,1,0:T(8,128)} copy(f32[4,4,128,8,256]{2,4,1,3,0:T(8,128)} %pad_maximum_fusion.6) | data formatting | bytes 33554432 | tf_op jit(solution)/shard_map/while/body/eval_jaxpr/concatenate | solution.py:48
  446.0 34.4 %scatter_fusion = f32[32,128,8,256]{3,2,1,0:T(8,128)} fusion(f32[32,128,8,256]{3,2,1,0:T(8,128)} %get-tuple-element.256, s32[16]{0:T(128)S(1)} %fusion.60, f32[16,128,8,256]{3,2,1,0:T(8,128)} %bitcast.144), kind=kCustom, calls=%fused_computation.2.clone.clone.1 | custom fusion | flops 4194304 | bytes 50331712 | tf_op jit(solution)/shard_map/while/body/eval_jaxpr/scatter-add | solution.py:94
  523.7 19.9 %copy.185 = f32[4,4,128,8,256]{4,3,2,1,0:T(8,128)} copy(f32[4,4,128,8,256]{2,4,1,3,0:T(8,128)} %pad_maximum_fusion.6) | data formatting | bytes 33554432 | tf_op jit(solution)/shard_map/while/body/eval_jaxpr/concatenate | solution.py:48
  543.6 34.4 %scatter_fusion = f32[32,128,8,256]{3,2,1,0:T(8,128)} fusion(f32[32,128,8,256]{3,2,1,0:T(8,128)} %get-tuple-element.256, s32[16]{0:T(128)S(1)} %fusion.60, f32[16,128,8,256]{3,2,1,0:T(8,128)} %bitcast.144), kind=kCustom, calls=%fused_computation.2.clone.clone.1 | custom fusion | flops 4194304 | bytes 50331712 | tf_op jit(solution)/shard_map/while/body/eval_jaxpr/scatter-add | solution.py:94
  580.6 10.6 gather_fusion.1
  621.4 19.9 %copy.185 = f32[4,4,128,8,256]{4,3,2,1,0:T(8,128)} copy(f32[4,4,128,8,256]{2,4,1,3,0:T(8,128)} %pad_maximum_fusion.6) | data formatting | bytes 33554432 | tf_op jit(solution)/shard_map/while/body/eval_jaxpr/concatenate | solution.py:48
  641.2 34.4 %scatter_fusion = f32[32,128,8,256]{3,2,1,0:T(8,128)} fusion(f32[32,128,8,256]{3,2,1,0:T(8,128)} %get-tuple-element.256, s32[16]{0:T(128)S(1)} %fusion.60, f32[16,128,8,256]{3,2,1,0:T(8,128)} %bitcast.144), kind=kCustom, calls=%fused_computation.2.clone.clone.1 | custom fusion | flops 4194304 | bytes 50331712 | tf_op jit(solution)/shard_map/while/body/eval_jaxpr/scatter-add | solution.py:94
  680.4 20.4 %convert.13 = bf16[32,128,8,256]{3,2,1,0:T(8,128)(2,1)} convert(f32[32,128,8,256]{3,2,1,0:T(8,128)} %get-tuple-element.52) | non-fusion elementwise | flops 8388608 | bytes 50331648 | tf_op jit(solution)/shard_map/convert.6
  721.9 82.9 %collective-permute-done.3 = bf16[1024,8,256]{2,1,0:T(8,128)(2,1)S(1)} collective-permute-done((bf16[1024,8,256]{2,1,0:T(8,128)(2,1)}, bf16[1024,8,256]{2,1,0:T(8,128)(2,1)S(1)}, u32[]{:S(2)}, u32[]{:S(2)}) %collective-permute-start.3) | collective-permute-done | bytes 4194336 | tf_op jit(solution)/shard_map/ppermute | solution.py:17
  806.8 88.4 %collective-permute-done.2 = bf16[1024,8,256]{2,1,0:T(8,128)(2,1)} collective-permute-done((bf16[1024,8,256]{2,1,0:T(8,128)(2,1)}, bf16[1024,8,256]{2,1,0:T(8,128)(2,1)}, u32[]{:S(2)}, u32[]{:S(2)}) %collective-permute-start.2) | collective-permute-done | bytes 4194336 | tf_op jit(solution)/shard_map/ppermute | solution.py:14
  895.2 15.4 %maximum_convert_fusion = (f32[1024,8,256]{2,1,0:T(8,128)}, f32[1024,8,256]{2,1,0:T(8,128)}) fusion(bf16[1024,8,256]{2,1,0:T(8,128)(2,1)} %copy-done.6, bf16[1024,8,256]{2,1,0:T(8,128)(2,1)} %bitcast.159, bf16[1024,8,256]{2,1,0:T(8,128)(2,1)} %bitcast.161, bf16[1024,8,256]{2,1,0:T(8,128)(2,1)} %collective-permute-done.2), kind=kLoop, calls=%fused_computation.55 | loop fusion | flops 16777216 | bytes 33554432 | tf_op jit(solution)/shard_map/slice | solution.py:115
  910.6 11.5 %fusion.32 = bf16[2048,8,256]{2,1,0:T(8,128)(2,1)} fusion(f32[1024,8,256]{2,1,0:T(8,128)} %get-tuple-element.167, f32[1024,8,256]{2,1,0:T(8,128)} %get-tuple-element.166, f32[16,128,8,256]{3,2,1,0:T(8,128)S(1)} %copy-done.1), kind=kLoop, calls=%fused_computation.48 | loop fusion | flops 12582912 | bytes 41943040 | tf_op jit(solution)/shard_map/convert.2
  928.0 98.9 %all_to_all.66 = bf16[2048,8,128]{2,1,0:T(8,128)(2,1)} all-to-all(bf16[2048,8,128]{2,1,0:T(8,128)(2,1)} %get-tuple-element.170), channel_id=1, replica_groups=mesh['seq'=4,'head'=8] {'head'}, dimensions={0} | all-to-all | bytes 8388608 | tf_op jit(solution)/shard_map/all_to_all | solution.py:122
  1060.6 64.8 %all-to-all-done.2 = bf16[2048,8,128]{2,1,0:T(8,128)(2,1)} async-done(((bf16[2048,8,128]{2,1,0:T(8,128)(2,1)}), bf16[2048,8,128]{2,1,0:T(8,128)(2,1)}, u32[]{:S(2)}, u32[]{:S(2)}) %all-to-all-start.2) | async-done | bytes 4194336 | tf_op jit(solution)/shard_map/all_to_all | solution.py:121
  (177 shorter events, 272.9 us)
Async XLA Ops:
  14.5 217.6 %all-to-all-start = ((bf16[256,64,128]{2,0,1:T(8,128)(2,1)}), bf16[256,64,128]{2,0,1:T(8,128)(2,1)}, u32[]{:S(2)}, u32[]{:S(2)}) async-start(bf16[256,64,128]{2,0,1:T(8,128)(2,1)} %copy.107), calls=%async_computation | async-start | bytes 8388608 | tf_op jit(solution)/shard_map/all_to_all | solution.py:63
  23.8 5.9 copy-start.2
  23.8 12.6 %copy-start.8 = (s32[64]{0:T(128)S(1)}, s32[64]{0:T(128)}, u32[]{:S(2)}) copy-start(s32[64]{0:T(128)} %param.15) | copy-start | bytes 772
  23.9 12.8 %copy-start.7 = (s32[64,4]{0,1:T(4,128)S(1)}, s32[64,4]{0,1:T(4,128)}, u32[]{:S(2)}) copy-start(s32[64,4]{0,1:T(4,128)} %param.14) | copy-start | bytes 3076
  29.7 96.5 %collective-permute-start = (bf16[1024,8,256]{2,1,0:T(8,128)(2,1)}, bf16[1024,8,256]{2,1,0:T(8,128)(2,1)}, u32[]{:S(2)}, u32[]{:S(2)}) collective-permute-start(bf16[1024,8,256]{2,1,0:T(8,128)(2,1)} %get-tuple-element.172), channel_id=1, source_target_pairs={{0,8},{8,16},{16,24},{1,9},{9,17},{17,25},{2,10},{10,18},{18,26},{... | collective-permute-start | bytes 12582920 | tf_op jit(solution)/shard_map/ppermute | solution.py:14
  33.1 180.7 %collective-permute-start.1 = (bf16[1024,8,256]{2,1,0:T(8,128)(2,1)}, bf16[1024,8,256]{2,1,0:T(8,128)(2,1)}, u32[]{:S(2)}, u32[]{:S(2)}) collective-permute-start(bf16[1024,8,256]{2,1,0:T(8,128)(2,1)} %get-tuple-element.173), channel_id=1, source_target_pairs={{8,0},{16,8},{24,16},{9,1},{17,9},{25,17},{10,2},{18,10},{26,18},{... | collective-permute-start | bytes 12582920 | tf_op jit(solution)/shard_map/ppermute | solution.py:17
  232.1 7.1 copy-start.5
  317.1 5.1 slice-start.8
  414.7 5.1 slice-start.8
  512.3 5.1 slice-start.8
  610.0 5.1 slice-start.8
  675.6 252.4 %all-to-all-start.1 = ((bf16[2048,8,128]{2,1,0:T(8,128)(2,1)}), bf16[2048,8,128]{2,1,0:T(8,128)(2,1)}, u32[]{:S(2)}, u32[]{:S(2)}) async-start(bf16[2048,8,128]{2,1,0:T(8,128)(2,1)} %bitcast.163), calls=%async_computation.1 | async-start | bytes 8388608 | tf_op jit(solution)/shard_map/all_to_all | solution.py:120
  680.3 35.2 %slice-start = ((s8[33554432]{0:T(1024)(128)(4,1)}), s8[4194304]{0:T(1024)(128)(4,1)S(1)}, s32[]{:S(2)}) async-start(s8[33554432]{0:T(1024)(128)(4,1)} %bitcast.145), calls=%async_computation.4 | async-start | bytes 8388608
  680.4 35.2 %slice-start.1 = ((s8[33554432]{0:T(1024)(128)(4,1)}), s8[4194304]{0:T(1024)(128)(4,1)S(1)}, s32[]{:S(2)}) async-start(s8[33554432]{0:T(1024)(128)(4,1)} %bitcast.145), calls=%async_computation.5 | async-start | bytes 8388608
  680.4 35.2 %slice-start.2 = ((s8[33554432]{0:T(1024)(128)(4,1)}), s8[4194304]{0:T(1024)(128)(4,1)S(1)}, s32[]{:S(2)}) async-start(s8[33554432]{0:T(1024)(128)(4,1)} %bitcast.145), calls=%async_computation.6 | async-start | bytes 8388608
  680.4 35.2 %slice-start.3 = ((s8[33554432]{0:T(1024)(128)(4,1)}), s8[4194304]{0:T(1024)(128)(4,1)S(1)}, s32[]{:S(2)}) async-start(s8[33554432]{0:T(1024)(128)(4,1)} %bitcast.145), calls=%async_computation.7 | async-start | bytes 8388608
  680.4 35.2 %slice-start.4 = ((s8[33554432]{0:T(1024)(128)(4,1)}), s8[4194304]{0:T(1024)(128)(4,1)S(1)}, s32[]{:S(2)}) async-start(s8[33554432]{0:T(1024)(128)(4,1)} %bitcast.145), calls=%async_computation.8 | async-start | bytes 8388608
  680.4 35.2 %slice-start.5 = ((s8[33554432]{0:T(1024)(128)(4,1)}), s8[4194304]{0:T(1024)(128)(4,1)S(1)}, s32[]{:S(2)}) async-start(s8[33554432]{0:T(1024)(128)(4,1)} %bitcast.145), calls=%async_computation.9 | async-start | bytes 8388608
  700.8 14.8 %slice-start.6 = ((s8[33554432]{0:T(1024)(128)(4,1)}), s8[4194304]{0:T(1024)(128)(4,1)S(1)}, s32[]{:S(2)}) async-start(s8[33554432]{0:T(1024)(128)(4,1)} %bitcast.145), calls=%async_computation.10 | async-start | bytes 8388608
  700.8 14.8 %slice-start.7 = ((s8[33554432]{0:T(1024)(128)(4,1)}), s8[4194304]{0:T(1024)(128)(4,1)S(1)}, s32[]{:S(2)}) async-start(s8[33554432]{0:T(1024)(128)(4,1)} %bitcast.145), calls=%async_computation.11 | async-start | bytes 8388608
  708.4 96.4 %collective-permute-start.3 = (bf16[1024,8,256]{2,1,0:T(8,128)(2,1)}, bf16[1024,8,256]{2,1,0:T(8,128)(2,1)S(1)}, u32[]{:S(2)}, u32[]{:S(2)}) collective-permute-start(bf16[1024,8,256]{2,1,0:T(8,128)(2,1)} %bitcast.160), channel_id=1, source_target_pairs={{8,0},{16,8},{24,16},{9,1},{17,9},{25,17},{10,2},{18,10},{26,18},{... | collective-permute-start | bytes 12582920 | tf_op jit(solution)/shard_map/ppermute | solution.py:17
  713.6 181.5 %collective-permute-start.2 = (bf16[1024,8,256]{2,1,0:T(8,128)(2,1)}, bf16[1024,8,256]{2,1,0:T(8,128)(2,1)}, u32[]{:S(2)}, u32[]{:S(2)}) collective-permute-start(bf16[1024,8,256]{2,1,0:T(8,128)(2,1)} %bitcast.158), channel_id=1, source_target_pairs={{0,8},{8,16},{16,24},{1,9},{9,17},{17,25},{2,10},{10,18},{18,26},{... | collective-permute-start | bytes 12582920 | tf_op jit(solution)/shard_map/ppermute | solution.py:14
  895.2 15.4 %copy-start.1 = (f32[16,128,8,256]{3,2,1,0:T(8,128)S(1)}, f32[16,128,8,256]{3,2,1,0:T(8,128)}, u32[]{:S(2)}) copy-start(f32[16,128,8,256]{3,2,1,0:T(8,128)} %slice.50) | copy-start | bytes 50331652
  1026.8 98.6 %all-to-all-start.2 = ((bf16[2048,8,128]{2,1,0:T(8,128)(2,1)}), bf16[2048,8,128]{2,1,0:T(8,128)(2,1)}, u32[]{:S(2)}, u32[]{:S(2)}) async-start(bf16[2048,8,128]{2,1,0:T(8,128)(2,1)} %get-tuple-element.171), calls=%async_computation.2 | async-start | bytes 8388608 | tf_op jit(solution)/shard_map/all_to_all | solution.py:121
  (11 other events, 32.4 us)
where the time goes:
time: 1140 us
  waiting for transfers between devices  413 us (36%)
  other arithmetic  271 us (24%)
  local copies, waits for them, and re-layouts  265 us (23%)
  blocking collectives  98.9 us (9%)
  matrix products  63.1 us (6%)
  starting transfers between devices  28 us (2%)
    ppermute x2, waiting for transfers between devices, with_halo(): lax.ppermute(lax.slice_in_dim(block, block.shape[dim] - width, None, axis...  177 us
    ppermute x2, waiting for transfers between devices, with_halo(): lax.ppermute(lax.slice_in_dim(block, 0, width, axis=dim), axis, backward)  170 us
    scatter-add x4, other arithmetic, own_step(): totals.at[list_blk.reshape(-1)]  138 us
    all_to_all x1, blocking collectives, per_device(): lax.all_to_all(grad_v, 'head', split_axis=0, concat_axis=1, tiled=True)  98.9 us
    concatenate x4, local copies, waits for them, and re-layouts, pair_block(): jnp.concatenate([dkey_terms, dvalue_terms], axis=-1)  79.5 us
    all_to_all x1, waiting for transfers between devices, per_device(): lax.all_to_all(grad_k, 'head', split_axis=0, concat_axis=1, tiled=True)  64.8 us
    gather x4, local copies, waits for them, and re-layouts, pair_block(): gathered = kv_tiles[lists]  42.2 us
    unnamed x38, local copies, waits for them, and re-layouts  40.6 us
  transfers between devices with their start and end apart: 7, of which 5 were waited for; matrix products, arithmetic and copies ran while one was open for 11% of the time, Pallas kernels for 0%

commit v1 on v0

v1 whole, which is shorter than its diff:
```python
import functools

import jax
import jax.numpy as jnp
from jax import lax
from jax.experimental import pallas as pl
from jax.experimental.pallas import tpu as pltpu
from jax.sharding import PartitionSpec as P

TILE = 128
CHUNKS = 4
NT = (((1,), (1,)), ((), ()))
TN = (((0,), (0,)), ((), ()))


def tile_load(ref, head, tile, piece):
    if piece >= TILE:
        per = piece // TILE
        rows = pl.ds(pl.multiple_of((tile % per) * TILE, TILE), TILE)
        return ref[tile // per, head, rows, :]
    per = TILE // piece
    return ref[pl.ds(tile * per, per), head, :, :].reshape(TILE, ref.shape[-1])


def tile_store(ref, head, tile, piece, value):
    if piece >= TILE:
        per = piece // TILE
        rows = pl.ds(pl.multiple_of((tile % per) * TILE, TILE), TILE)
        ref[tile // per, head, rows, :] = value
    else:
        per = TILE // piece
        ref[pl.ds(tile * per, per), head, :, :] = value.reshape(per, piece, ref.shape[-1])


def attention_kernel(
    piece, lists, key_counts, query_counts,
    q_ref, o_ref, g_ref, low_ref, own_low_ref, own_high_ref, high_ref,
    dq_ref, mid_ref, flank_low_ref, flank_high_ref,
    k_ext, v_ext, k_acc, v_acc,
):
    heads, tokens, head_dim = q_ref.shape
    half = tokens // 2
    scale = head_dim ** (-0.5)
    nbr = lists.shape[0] // (tokens // TILE)
    for place, ref in enumerate((low_ref, own_low_ref, own_high_ref, high_ref)):
        k_ext[:, place * half : (place + 1) * half, :] = ref[0]
        v_ext[:, place * half : (place + 1) * half, :] = ref[1]
    k_acc[...] = jnp.zeros_like(k_acc)
    v_acc[...] = jnp.zeros_like(v_acc)
    row = lax.broadcasted_iota(jnp.int32, (TILE, TILE), 0)

    def step(tile, carry):
        picks = [lists[tile * nbr + n] for n in range(nbr)]
        spots = [pl.ds(pl.multiple_of(pick * TILE, TILE), TILE) for pick in picks]
        limits = [key_counts[pick] for pick in picks]
        own_rows = pl.ds(pl.multiple_of(tile * TILE, TILE), TILE)
        query_live = row[:, :head_dim] < query_counts[tile]
        for head in range(heads):
            query = q_ref[head, own_rows, :]
            grad_f = jnp.where(query_live, tile_load(g_ref, head, tile, piece).astype(jnp.float32), 0.0)
            grad = grad_f.astype(jnp.bfloat16)
            product = grad_f * o_ref[head, own_rows, :].astype(jnp.float32)
            delta = jnp.sum(product.T, axis=0, keepdims=True)
            keys = jnp.concatenate([k_ext[head, spot, :] for spot in spots], axis=0)
            values = jnp.concatenate([v_ext[head, spot, :] for spot in spots], axis=0)
            scores = lax.dot_general(keys, query, NT, preferred_element_type=jnp.float32) * scale
            scores = jnp.concatenate(
                [
                    jnp.where(row < limits[n], scores[n * TILE : (n + 1) * TILE], -1e30)
                    for n in range(nbr)
                ],
                axis=0,
            )
            top = jnp.max(scores, axis=0, keepdims=True)
            weights = jnp.exp(scores - top)
            probs = weights * (1.0 / jnp.sum(weights, axis=0, keepdims=True))
            dprobs = lax.dot_general(values, grad, NT, preferred_element_type=jnp.float32)
            dscore = (probs * (dprobs - delta) * scale).astype(jnp.bfloat16)
            probs_low = probs.astype(jnp.bfloat16)
            dquery = lax.dot_general(dscore, keys, TN, preferred_element_type=jnp.float32)
            dkey = jnp.dot(dscore, query, preferred_element_type=jnp.float32)
            dvalue = jnp.dot(probs_low, grad, preferred_element_type=jnp.float32)
            tile_store(dq_ref, head, tile, piece, dquery.astype(jnp.bfloat16))
            for n, spot in enumerate(spots):
                k_acc[head, spot, :] += dkey[n * TILE : (n + 1) * TILE]
                v_acc[head, spot, :] += dvalue[n * TILE : (n + 1) * TILE]
        return carry

    lax.fori_loop(0, tokens // TILE, step, 0)
    pieces = half // piece
    for which, acc in enumerate((k_acc, v_acc)):
        for head in range(heads):
            for ref, start, count in (
                (flank_low_ref, 0, pieces),
                (mid_ref, half, 2 * pieces),
                (flank_high_ref, 3 * half, pieces),
            ):
                part = acc[head, start : start + count * piece, :].astype(jnp.bfloat16)
                ref[:, which, head, :, :] = part.reshape(count, piece, head_dim)


def attention(lists, key_counts, query_counts, q, o, g, low, own_low, own_high, high, first):
    heads, tokens, head_dim = q.shape
    groups, here, piece, _ = g.shape
    half_groups = groups // 2
    step = 2 if here % 2 == 0 else 1
    half = tokens // 2
    nbr = lists.shape[0] // (tokens // TILE)
    rows = pl.BlockSpec((step, tokens, head_dim), lambda i, *_: (i + first // step, 0, 0))
    pieces = pl.BlockSpec((groups, step, piece, head_dim), lambda i, *_: (0, i, 0, 0))
    halves = pl.BlockSpec((2, step, half, head_dim), lambda i, *_: (0, i, 0, 0))

    def outs(count):
        return pl.BlockSpec((count, 2, step, piece, head_dim), lambda i, *_: (0, 0, i, 0, 0))

    def made(*shape):
        return jax.ShapeDtypeStruct(shape, jnp.bfloat16)

    pairs = here * (tokens // TILE) * nbr
    return pl.pallas_call(
        functools.partial(attention_kernel, piece),
        out_shape=(
            made(groups, here, piece, head_dim),
            made(groups, 2, here, piece, head_dim),
            made(half_groups, 2, here, piece, head_dim),
            made(half_groups, 2, here, piece, head_dim),
        ),
        grid_spec=pltpu.PrefetchScalarGridSpec(
            num_scalar_prefetch=3,
            grid=(here // step,),
            in_specs=[rows, rows, pieces, halves, halves, halves, halves],
            out_specs=[pieces, outs(groups), outs(half_groups), outs(half_groups)],
            scratch_shapes=[
                pltpu.VMEM((step, 2 * tokens, head_dim), jnp.bfloat16),
                pltpu.VMEM((step, 2 * tokens, head_dim), jnp.bfloat16),
                pltpu.VMEM((step, 2 * tokens, head_dim), jnp.float32),
                pltpu.VMEM((step, 2 * tokens, head_dim), jnp.float32),
            ],
        ),
        compiler_params=pltpu.CompilerParams(vmem_limit_bytes=52 * 2**20),
        cost_estimate=pl.CostEstimate(
            flops=pairs * 10 * TILE * TILE * head_dim * 4,
            bytes_accessed=here * tokens * head_dim * 2 * 12,
            transcendentals=pairs * TILE * TILE,
        ),
    )(lists, key_counts, query_counts, q, o, g, low, own_low, own_high, high)


def after(value, earlier):
    if earlier is None:
        return value
    return lax.optimization_barrier((value, earlier))[0]


def shift(value, up):
    count = lax.axis_size("seq")
    pairs = [(i, i + 1) if up else (i + 1, i) for i in range(count - 1)]
    return lax.ppermute(value, "seq", pairs)


def exchange(value):
    return lax.all_to_all(value, "head", split_axis=0, concat_axis=0, tiled=True)


def per_device(query_rows, key_rows, value_rows, attn_output, out_grad, neighbours, counts):
    seq_rows, batch, width = out_grad.shape
    tokens, heads, head_dim = query_rows.shape
    groups = lax.axis_size("head")
    nbr = neighbours.shape[1]
    tiles = tokens // TILE
    half = tokens // 2
    chunks = min(CHUNKS, heads)
    here = heads // chunks

    first_tile = lax.axis_index("seq") * tiles
    ext_base = first_tile - tiles // 2
    lists = lax.dynamic_slice_in_dim(neighbours, first_tile, tiles, 0) - ext_base
    lists = jnp.clip(lists, 0, 2 * tiles - 1).reshape(-1)
    padded = jnp.pad(counts, (tiles // 2, tiles // 2))
    key_counts = lax.dynamic_slice_in_dim(padded, first_tile, 2 * tiles, 0)
    query_counts = lax.dynamic_slice_in_dim(counts, first_tile, tiles, 0)

    def kv_half(c, start):
        cut = [
            jnp.swapaxes(a[start : start + half, c * here : (c + 1) * here, :], 0, 1)
            for a in (key_rows, value_rows)
        ]
        return jnp.stack(cut)

    q = jnp.swapaxes(query_rows, 0, 1)
    o = jnp.swapaxes(attn_output, 0, 1)
    grads = jnp.swapaxes(out_grad.reshape(seq_rows, groups, heads, head_dim), 0, 1)
    grads = jnp.swapaxes(grads, 1, 2)

    dq_parts, dkv_parts = [], []
    halo = None
    for c in range(chunks):
        own_low, own_high = kv_half(c, 0), kv_half(c, half)
        send_low, send_high = after((own_low, own_high), halo)
        low, high = shift(send_high, True), shift(send_low, False)
        halo = (low, high)
        g = exchange(grads[:, c * here : (c + 1) * here])
        dq, mid, flank_low, flank_high = attention(
            lists, key_counts, query_counts, q, o, g, low, own_low, own_high, high, c * here
        )
        from_low, from_high = shift(flank_high, True), shift(flank_low, False)
        dq_parts.append(exchange(dq))
        returned = jnp.concatenate([from_low, from_high], axis=0).astype(jnp.float32)
        total = (mid.astype(jnp.float32) + returned).astype(jnp.bfloat16)
        dkv_parts.append(exchange(total))

    def finish(parts):
        whole = jnp.stack(parts, axis=1).reshape(groups * heads, seq_rows, head_dim)
        return jnp.swapaxes(whole, 0, 1).reshape(seq_rows, batch, width)

    return (
        finish(dq_parts),
        finish([part[:, 0] for part in dkv_parts]),
        finish([part[:, 1] for part in dkv_parts]),
    )


def solution(mesh):
    rows = P("seq", "head", None)
    pieces = P(("seq", "head"), None, None)
    return jax.shard_map(
        per_device,
        mesh=mesh,
        in_specs=(rows, rows, rows, rows, pieces, P(), P()),
        out_specs=(pieces, pieces, pieces),
        check_vma=False,
    )
```

time: 1140 us -> 618 us (0.54)
  other arithmetic: 271 us -> 29.3 us
  waiting for transfers between devices: 413 us -> 241 us
  local copies, waits for them, and re-layouts: 265 us -> 100 us
  Pallas kernels: 0 us -> 101 us
  starting transfers between devices: 28 us -> 106 us
  blocking collectives: 98.9 us -> 31.4 us
  matrix products: 63.1 us -> 0 us
    ppermute x4 -> x16, waiting for transfers between devices: 348 us -> 197 us  [shift(): return lax.ppermute(value, 'seq', pairs)]
    scatter-add x4 -> x0, other arithmetic: 138 us -> none  [own_step(): totals.at[list_blk.reshape(-1)]]
    pallas_call x0 -> x4, Pallas kernels: none -> 101 us  [attention(): pl.pallas_call(functools.partial(attention_kernel, piece), out_shape=(mad...]
    concatenate x5 -> x0, local copies, waits for them, and re-layouts: 80.5 us -> none  [the longest x4 79.5 us: pair_block(): jnp.concatenate([dkey_terms, dvalue_terms], axis=-1)]
    all_to_all x1, blocking collectives: 98.9 us -> 31.4 us  [exchange(): lax.all_to_all(value, 'head', split_axis=0, concat_axis=0, tiled=True)]
    dot_general x20 -> x0, matrix products: 63.1 us -> none  [the longest x4 19 us: pair_block(): jnp.einsum('icgnj,icgd->injgd', probs_low, grad_rows, preferred_element_t...]
    gather x8 -> x0, local copies, waits for them, and re-layouts: 44.6 us -> none  [the longest x4 42.2 us: pair_block(): gathered = kv_tiles[lists]]
    ppermute x4 -> x16, starting transfers between devices: 13.9 us -> 57.5 us  [shift(): return lax.ppermute(value, 'seq', pairs)]
  transfers between devices with their start and end apart: 7 -> 27, of which waited for: 5 -> 15; matrix products, arithmetic and copies ran while one was open for 11% -> 13% of each run, Pallas kernels for 0% -> 17%
where the time goes in v1:
time: 618 us; the launch traced here: 610 us
  waiting for transfers between devices  241 us (39%)
  starting transfers between devices  106 us (17%)
  Pallas kernels  101 us (16%)
  local copies, waits for them, and re-layouts  100 us (16%)
  blocking collectives  31.4 us (5%)
  other arithmetic  29.3 us (5%)
    ppermute x16, waiting for transfers between devices, shift(): return lax.ppermute(value, 'seq', pairs)  197 us
    pallas_call x4, Pallas kernels, attention(): pl.pallas_call(functools.partial(attention_kernel, piece), out_shape=(mad...  101 us
    ppermute x16, starting transfers between devices, shift(): return lax.ppermute(value, 'seq', pairs)  57.5 us
    all_to_all x11, starting transfers between devices, exchange(): lax.all_to_all(value, 'head', split_axis=0, concat_axis=0, tiled=True)  48.7 us
    all_to_all x11, waiting for transfers between devices, exchange(): lax.all_to_all(value, 'head', split_axis=0, concat_axis=0, tiled=True)  44.4 us
    all_to_all x1, blocking collectives, exchange(): lax.all_to_all(value, 'head', split_axis=0, concat_axis=0, tiled=True)  31.4 us
    unnamed x26, local copies, waits for them, and re-layouts  17.3 us
    transpose x3, local copies, waits for them, and re-layouts, finish(): return jnp.swapaxes(whole, 0, 1).reshape(seq_rows, batch, width)  15.8 us
  transfers between devices with their start and end apart: 27, of which 15 were waited for; matrix products, arithmetic and copies ran while one was open for 13% of the time, Pallas kernels for 17%

profile of v1, /device:TPU:4, one launch (start us, length us, event | category | flops | bytes accessed | tf_op | source)
XLA Modules:
  0.0 610.2 jit_solution(808927847196954756)
XLA Ops:
  0.6 7.5 %copy.58 = bf16[256,4,2048]{0,2,1:T(8,128)(2,1)} copy(bf16[256,4,2048]{2,1,0:T(4,128)(2,1)} %param.11) | data formatting | bytes 8388608 | tf_op args[4]
  18.5 31.4 %all_to_all.60.g_ref = bf16[8,2,256,128]{3,2,1,0:T(8,128)(2,1)} all-to-all(bf16[8,2,256,128]{3,2,1,0:T(8,128)(2,1)S(1)} %get-tuple-element.50), channel_id=1, replica_groups=mesh['seq'=4,'head'=8] {'head'}, dimensions={0} | all-to-all | bytes 2097152 | tf_op jit(solution)/shard_map/all_to_all | solution.py:162
  54.2 11.3 %fusion.1 = (bf16[1024,2,128]{2,1,0:T(2,128)(2,1)}, bf16[1024,2,128]{2,1,0:T(2,128)(2,1)S(1)}, bf16[1024,2,128]{2,1,0:T(2,128)(2,1)S(1)}, bf16[1024,2,128]{2,1,0...) fusion(bf16[2048,8,128]{2,1,0:T(8,128)(2,1)} %param.8), kind=kLoop, calls=%fused_computation.36 | loop fusion | bytes 8388608 | tf_op jit(solution)/shard_map/slice | solution.py:185
  69.9 10.9 %all-to-all-done.2.g_ref = bf16[8,2,256,128]{3,2,1,0:T(8,128)(2,1)} async-done(((bf16[8,2,256,128]{3,2,1,0:T(8,128)(2,1)}), bf16[8,2,256,128]{3,2,1,0:T(8,128)(2,1)}, u32[]{:S(2)}, u32[]{:S(2)}) %all-to-all-start.2) | async-done | bytes 1048608 | tf_op jit(solution)/shard_map/all_to_all | solution.py:162
  102.1 9.5 %all-to-all-done.4.g_ref = bf16[8,2,256,128]{3,2,1,0:T(8,128)(2,1)} async-done(((bf16[8,2,256,128]{3,2,1,0:T(8,128)(2,1)}), bf16[8,2,256,128]{3,2,1,0:T(8,128)(2,1)}, u32[]{:S(2)}, u32[]{:S(2)}) %all-to-all-start.4) | async-done | bytes 1048608 | tf_op jit(solution)/shard_map/all_to_all | solution.py:162
  115.2 6.6 %copy_bitcast_fusion = (bf16[8,2048,128]{2,1,0:T(8,128)(2,1)}, bf16[8,2048,128]{2,1,0:T(8,128)(2,1)}) fusion(bf16[2048,8,128]{2,1,0:T(8,128)(2,1)} %param.10, bf16[2048,8,128]{2,1,0:T(8,128)(2,1)} %param.7), kind=kLoop, calls=%fused_computation.3 | loop fusion | bytes 16777216 | tf_op jit(solution)/shard_map/transpose | solution.py:191
  121.8 14.8 %collective-permute-done.1.high_ref = bf16[2,2,1024,128]{3,2,1,0:T(8,128)(2,1)} collective-permute-done((bf16[2,2,1024,128]{3,2,1,0:T(8,128)(2,1)}, bf16[2,2,1024,128]{3,2,1,0:T(8,128)(2,1)}, u32[]{:S(2)}, u32[]{:S(2)}) %collective-permute-start.1) | collective-permute-done | bytes 1048608 | tf_op jit(solution)/shard_map/ppermute | solution.py:158
  143.8 25.2 %shard_map.94 = (bf16[8,2,256,128]{3,2,1,0:T(8,128)(2,1)}, bf16[8,2,2,256,128]{4,3,2,1,0:T(8,128)(2,1)}, bf16[4,2,2,256,128]{4,3,2,1,0:T(8,128)(2,1)}, bf16[4,2,2,256,128]{4,3,2,1,0:T(8,128)(2,1)}) custom-call(s32[64]{0:T(128)S(1)} %reshape.30.lists, s32[32]{0:T(128)S(1)} %pad_dynamic-slice_fusion.key_counts, s32[16]{0:T(128)S(1)} %dynamic_slice.11.query_counts, ...), custom_call_target="tpu_custom_call" | custom-call | flops 10737418240 | bytes 12582912 | tf_op jit(solution)/shard_map/pallas_call | solution.py:120
  191.1 25.1 %shard_map.95 = (bf16[8,2,256,128]{3,2,1,0:T(8,128)(2,1)}, bf16[8,2,2,256,128]{4,3,2,1,0:T(8,128)(2,1)}, bf16[4,2,2,256,128]{4,3,2,1,0:T(8,128)(2,1)}, bf16[4,2,2,256,128]{4,3,2,1,0:T(8,128)(2,1)}) custom-call(s32[64]{0:T(128)S(1)} %reshape.30.lists, s32[32]{0:T(128)S(1)} %pad_dynamic-slice_fusion.key_counts, s32[16]{0:T(128)S(1)} %dynamic_slice.11.query_counts, ...), custom_call_target="tpu_custom_call" | custom-call | flops 10737418240 | bytes 12582912 | tf_op jit(solution)/shard_map/pallas_call | solution.py:120
  237.4 25.2 %shard_map.96 = (bf16[8,2,256,128]{3,2,1,0:T(8,128)(2,1)}, bf16[8,2,2,256,128]{4,3,2,1,0:T(8,128)(2,1)}, bf16[4,2,2,256,128]{4,3,2,1,0:T(8,128)(2,1)}, bf16[4,2,2,256,128]{4,3,2,1,0:T(8,128)(2,1)}) custom-call(s32[64]{0:T(128)S(1)} %reshape.30.lists, s32[32]{0:T(128)S(1)} %pad_dynamic-slice_fusion.key_counts, s32[16]{0:T(128)S(1)} %dynamic_slice.11.query_counts, ...), custom_call_target="tpu_custom_call" | custom-call | flops 10737418240 | bytes 12582912 | tf_op jit(solution)/shard_map/pallas_call | solution.py:120
  266.9 9.1 %collective-permute-done.7.high_ref = bf16[2,2,1024,128]{3,2,1,0:T(8,128)(2,1)} collective-permute-done((bf16[2,2,1024,128]{3,2,1,0:T(8,128)(2,1)}, bf16[2,2,1024,128]{3,2,1,0:T(8,128)(2,1)}, u32[]{:S(2)}, u32[]{:S(2)}) %collective-permute-start.7) | collective-permute-done | bytes 1048608 | tf_op jit(solution)/shard_map/ppermute | solution.py:158
  276.1 25.3 %shard_map.97 = (bf16[8,2,256,128]{3,2,1,0:T(8,128)(2,1)}, bf16[8,2,2,256,128]{4,3,2,1,0:T(8,128)(2,1)}, bf16[4,2,2,256,128]{4,3,2,1,0:T(8,128)(2,1)}, bf16[4,2,2,256,128]{4,3,2,1,0:T(8,128)(2,1)}) custom-call(s32[64]{0:T(128)S(1)} %reshape.30.lists, s32[32]{0:T(128)S(1)} %pad_dynamic-slice_fusion.key_counts, s32[16]{0:T(128)S(1)} %dynamic_slice.11.query_counts, ...), custom_call_target="tpu_custom_call" | custom-call | flops 10737418240 | bytes 12582912 | tf_op jit(solution)/shard_map/pallas_call | solution.py:120
  312.6 22.3 %collective-permute-done.8 = bf16[4,2,2,256,128]{4,3,2,1,0:T(8,128)(2,1)S(1)} collective-permute-done((bf16[4,2,2,256,128]{4,3,2,1,0:T(8,128)(2,1)}, bf16[4,2,2,256,128]{4,3,2,1,0:T(8,128)(2,1)S(1)}, u32[]{:S(2)}, u32[]{:S(2)}) %collective-permute-start.8) | collective-permute-done | bytes 1048608 | tf_op jit(solution)/shard_map/ppermute | solution.py:158
  334.9 18.6 %collective-permute-done.9 = bf16[4,2,2,256,128]{4,3,2,1,0:T(8,128)(2,1)S(1)} collective-permute-done((bf16[4,2,2,256,128]{4,3,2,1,0:T(8,128)(2,1)}, bf16[4,2,2,256,128]{4,3,2,1,0:T(8,128)(2,1)S(1)}, u32[]{:S(2)}, u32[]{:S(2)}) %collective-permute-start.9) | collective-permute-done | bytes 1048608 | tf_op jit(solution)/shard_map/ppermute | solution.py:158
  370.1 22.3 %collective-permute-done.10 = bf16[4,2,2,256,128]{4,3,2,1,0:T(8,128)(2,1)S(1)} collective-permute-done((bf16[4,2,2,256,128]{4,3,2,1,0:T(8,128)(2,1)}, bf16[4,2,2,256,128]{4,3,2,1,0:T(8,128)(2,1)S(1)}, u32[]{:S(2)}, u32[]{:S(2)}) %collective-permute-start.10) | collective-permute-done | bytes 1048608 | tf_op jit(solution)/shard_map/ppermute | solution.py:158
  392.4 18.6 %collective-permute-done.11 = bf16[4,2,2,256,128]{4,3,2,1,0:T(8,128)(2,1)S(1)} collective-permute-done((bf16[4,2,2,256,128]{4,3,2,1,0:T(8,128)(2,1)}, bf16[4,2,2,256,128]{4,3,2,1,0:T(8,128)(2,1)S(1)}, u32[]{:S(2)}, u32[]{:S(2)}) %collective-permute-start.11) | collective-permute-done | bytes 1048608 | tf_op jit(solution)/shard_map/ppermute | solution.py:158
  426.7 22.3 %collective-permute-done.12 = bf16[4,2,2,256,128]{4,3,2,1,0:T(8,128)(2,1)S(1)} collective-permute-done((bf16[4,2,2,256,128]{4,3,2,1,0:T(8,128)(2,1)}, bf16[4,2,2,256,128]{4,3,2,1,0:T(8,128)(2,1)S(1)}, u32[]{:S(2)}, u32[]{:S(2)}) %collective-permute-start.12) | collective-permute-done | bytes 1048608 | tf_op jit(solution)/shard_map/ppermute | solution.py:158
  449.0 18.6 %collective-permute-done.13 = bf16[4,2,2,256,128]{4,3,2,1,0:T(8,128)(2,1)S(1)} collective-permute-done((bf16[4,2,2,256,128]{4,3,2,1,0:T(8,128)(2,1)}, bf16[4,2,2,256,128]{4,3,2,1,0:T(8,128)(2,1)S(1)}, u32[]{:S(2)}, u32[]{:S(2)}) %collective-permute-start.13) | collective-permute-done | bytes 1048608 | tf_op jit(solution)/shard_map/ppermute | solution.py:158
  483.6 22.1 %collective-permute-done.14 = bf16[4,2,2,256,128]{4,3,2,1,0:T(8,128)(2,1)S(1)} collective-permute-done((bf16[4,2,2,256,128]{4,3,2,1,0:T(8,128)(2,1)}, bf16[4,2,2,256,128]{4,3,2,1,0:T(8,128)(2,1)S(1)}, u32[]{:S(2)}, u32[]{:S(2)}) %collective-permute-start.14) | collective-permute-done | bytes 1048608 | tf_op jit(solution)/shard_map/ppermute | solution.py:158
  505.6 18.6 %collective-permute-done.15 = bf16[4,2,2,256,128]{4,3,2,1,0:T(8,128)(2,1)S(1)} collective-permute-done((bf16[4,2,2,256,128]{4,3,2,1,0:T(8,128)(2,1)}, bf16[4,2,2,256,128]{4,3,2,1,0:T(8,128)(2,1)S(1)}, u32[]{:S(2)}, u32[]{:S(2)}) %collective-permute-start.15) | collective-permute-done | bytes 1048608 | tf_op jit(solution)/shard_map/ppermute | solution.py:158
  543.6 7.8 %copy.80 = bf16[256,4,2048]{2,1,0:T(4,128)(2,1)} copy(bf16[256,4,2048]{0,2,1:T(8,128)(2,1)} %bitcast.88) | data formatting | bytes 8388608
  558.0 24.0 %all-to-all-done.11 = bf16[8,2,2,256,128]{4,3,2,1,0:T(8,128)(2,1)} async-done(((bf16[8,2,2,256,128]{4,3,2,1,0:T(8,128)(2,1)}), bf16[8,2,2,256,128]{4,3,2,1,0:T(8,128)(2,1)}, u32[]{:S(2)}, u32[]{:S(2)}) %all-to-all-start.11) | async-done | bytes 2097184 | tf_op jit(solution)/shard_map/all_to_all | solution.py:162
  590.2 6.9 %reshape.37 = bf16[256,4,2048]{2,1,0:T(4,128)(2,1)} reshape(bf16[256,64,128]{2,1,0:T(8,128)(2,1)} %copy.79) | data formatting | bytes 8388608 | tf_op jit(solution)/shard_map/reshape | solution.py:214
  603.4 6.9 %reshape.35 = bf16[256,4,2048]{2,1,0:T(4,128)(2,1)} reshape(bf16[256,64,128]{2,1,0:T(8,128)(2,1)} %copy.78) | data formatting | bytes 8388608 | tf_op jit(solution)/shard_map/reshape | solution.py:214
  (104 shorter events, 198.6 us)
Async XLA Ops:
  49.9 30.8 %all-to-all-start.2 = ((bf16[8,2,256,128]{3,2,1,0:T(8,128)(2,1)}), bf16[8,2,256,128]{3,2,1,0:T(8,128)(2,1)}, u32[]{:S(2)}, u32[]{:S(2)}) async-start(bf16[8,2,256,128]{3,2,1,0:T(8,128)(2,1)} %get-tuple-element.53), calls=%async_computation.2 | async-start | bytes 2097152 | tf_op jit(solution)/shard_map/all_to_all | solution.py:162
  80.7 30.8 %all-to-all-start.4 = ((bf16[8,2,256,128]{3,2,1,0:T(8,128)(2,1)}), bf16[8,2,256,128]{3,2,1,0:T(8,128)(2,1)}, u32[]{:S(2)}, u32[]{:S(2)}) async-start(bf16[8,2,256,128]{3,2,1,0:T(8,128)(2,1)} %get-tuple-element.52), calls=%async_computation.4 | async-start | bytes 2097152 | tf_op jit(solution)/shard_map/all_to_all | solution.py:162
  87.5 34.3 %collective-permute-start = (bf16[2,2,1024,128]{3,2,1,0:T(8,128)(2,1)}, bf16[2,2,1024,128]{3,2,1,0:T(8,128)(2,1)}, u32[]{:S(2)}, u32[]{:S(2)}) collective-permute-start(bf16[2,2,1024,128]{3,2,1,0:T(8,128)(2,1)} %pad_maximum_fusion.3.own_high_ref), channel_id=1, source_target_pairs={{0,8},{8,16},{16,24},{1,9},{9,17},{17,25},{2,10},{10,18},{18,26},{... | collective-permute-start | bytes 3145736 | tf_op jit(solution)/shard_map/ppermute | solution.py:158
  92.2 44.4 %collective-permute-start.1 = (bf16[2,2,1024,128]{3,2,1,0:T(8,128)(2,1)}, bf16[2,2,1024,128]{3,2,1,0:T(8,128)(2,1)}, u32[]{:S(2)}, u32[]{:S(2)}) collective-permute-start(bf16[2,2,1024,128]{3,2,1,0:T(8,128)(2,1)} %pad_maximum_fusion.4.own_low_ref), channel_id=1, source_target_pairs={{8,0},{16,8},{24,16},{9,1},{17,9},{25,17},{10,2},{18,10},{26,18},{... | collective-permute-start | bytes 3145736 | tf_op jit(solution)/shard_map/ppermute | solution.py:158
  111.6 57.5 %all-to-all-start.6 = ((bf16[8,2,256,128]{3,2,1,0:T(8,128)(2,1)}), bf16[8,2,256,128]{3,2,1,0:T(8,128)(2,1)S(1)}, u32[]{:S(2)}, u32[]{:S(2)}) async-start(bf16[8,2,256,128]{3,2,1,0:T(8,128)(2,1)} %get-tuple-element.51), calls=%async_computation.6 | async-start | bytes 2097152 | tf_op jit(solution)/shard_map/all_to_all | solution.py:162
  136.6 41.8 %collective-permute-start.2 = (bf16[2,2,1024,128]{3,2,1,0:T(8,128)(2,1)}, bf16[2,2,1024,128]{3,2,1,0:T(8,128)(2,1)}, u32[]{:S(2)}, u32[]{:S(2)}) collective-permute-start(bf16[2,2,1024,128]{3,2,1,0:T(8,128)(2,1)} %pad_maximum_fusion.6.own_high_ref), channel_id=1, source_target_pairs={{0,8},{8,16},{16,24},{1,9},{9,17},{17,25},{2,10},{10,18},{18,26},{... | collective-permute-start | bytes 3145736 | tf_op jit(solution)/shard_map/ppermute | solution.py:158
  138.5 45.2 %collective-permute-start.3 = (bf16[2,2,1024,128]{3,2,1,0:T(8,128)(2,1)}, bf16[2,2,1024,128]{3,2,1,0:T(8,128)(2,1)}, u32[]{:S(2)}, u32[]{:S(2)}) collective-permute-start(bf16[2,2,1024,128]{3,2,1,0:T(8,128)(2,1)} %pad_maximum_fusion.5.own_low_ref), channel_id=1, source_target_pairs={{8,0},{16,8},{24,16},{9,1},{17,9},{25,17},{10,2},{18,10},{26,18},{... | collective-permute-start | bytes 3145736 | tf_op jit(solution)/shard_map/ppermute | solution.py:158
  170.1 46.2 %all-to-all-start.1 = ((bf16[8,2,256,128]{3,2,1,0:T(8,128)(2,1)}), bf16[8,2,256,128]{3,2,1,0:T(8,128)(2,1)S(1)}, u32[]{:S(2)}, u32[]{:S(2)}) async-start(bf16[8,2,256,128]{3,2,1,0:T(8,128)(2,1)} %get-tuple-element.25), calls=%async_computation.1 | async-start | bytes 2097152 | tf_op jit(solution)/shard_map/all_to_all | solution.py:162
  183.7 41.8 %collective-permute-start.4 = (bf16[2,2,1024,128]{3,2,1,0:T(8,128)(2,1)}, bf16[2,2,1024,128]{3,2,1,0:T(8,128)(2,1)}, u32[]{:S(2)}, u32[]{:S(2)}) collective-permute-start(bf16[2,2,1024,128]{3,2,1,0:T(8,128)(2,1)} %pad_maximum_fusion.8.own_high_ref), channel_id=1, source_target_pairs={{0,8},{8,16},{16,24},{1,9},{9,17},{17,25},{2,10},{10,18},{18,26},{... | collective-permute-start | bytes 3145736 | tf_op jit(solution)/shard_map/ppermute | solution.py:158
  185.6 44.6 %collective-permute-start.5 = (bf16[2,2,1024,128]{3,2,1,0:T(8,128)(2,1)}, bf16[2,2,1024,128]{3,2,1,0:T(8,128)(2,1)}, u32[]{:S(2)}, u32[]{:S(2)}) collective-permute-start(bf16[2,2,1024,128]{3,2,1,0:T(8,128)(2,1)} %pad_maximum_fusion.7.own_low_ref), channel_id=1, source_target_pairs={{8,0},{16,8},{24,16},{9,1},{17,9},{25,17},{10,2},{18,10},{26,18},{... | collective-permute-start | bytes 3145736 | tf_op jit(solution)/shard_map/ppermute | solution.py:158
  216.2 46.4 %all-to-all-start.3 = ((bf16[8,2,256,128]{3,2,1,0:T(8,128)(2,1)}), bf16[8,2,256,128]{3,2,1,0:T(8,128)(2,1)S(1)}, u32[]{:S(2)}, u32[]{:S(2)}) async-start(bf16[8,2,256,128]{3,2,1,0:T(8,128)(2,1)} %get-tuple-element.28), calls=%async_computation.3 | async-start | bytes 2097152 | tf_op jit(solution)/shard_map/all_to_all | solution.py:162
  230.2 36.7 %collective-permute-start.6 = (bf16[2,2,1024,128]{3,2,1,0:T(8,128)(2,1)}, bf16[2,2,1024,128]{3,2,1,0:T(8,128)(2,1)}, u32[]{:S(2)}, u32[]{:S(2)}) collective-permute-start(bf16[2,2,1024,128]{3,2,1,0:T(8,128)(2,1)} %pad_maximum_fusion.10.own_high_ref), channel_id=1, source_target_pairs={{0,8},{8,16},{16,24},{1,9},{9,17},{17,25},{2,10},{10,18},{18,26},{... | collective-permute-start | bytes 3145736 | tf_op jit(solution)/shard_map/ppermute | solution.py:158
  232.1 43.9 %collective-permute-start.7 = (bf16[2,2,1024,128]{3,2,1,0:T(8,128)(2,1)}, bf16[2,2,1024,128]{3,2,1,0:T(8,128)(2,1)}, u32[]{:S(2)}, u32[]{:S(2)}) collective-permute-start(bf16[2,2,1024,128]{3,2,1,0:T(8,128)(2,1)} %pad_maximum_fusion.9.own_low_ref), channel_id=1, source_target_pairs={{8,0},{16,8},{24,16},{9,1},{17,9},{25,17},{10,2},{18,10},{26,18},{... | collective-permute-start | bytes 3145736 | tf_op jit(solution)/shard_map/ppermute | solution.py:158
  262.6 38.7 %all-to-all-start.5 = ((bf16[8,2,256,128]{3,2,1,0:T(8,128)(2,1)}), bf16[8,2,256,128]{3,2,1,0:T(8,128)(2,1)}, u32[]{:S(2)}, u32[]{:S(2)}) async-start(bf16[8,2,256,128]{3,2,1,0:T(8,128)(2,1)} %get-tuple-element.31), calls=%async_computation.5 | async-start | bytes 2097152 | tf_op jit(solution)/shard_map/all_to_all | solution.py:162
  301.3 55.9 %all-to-all-start.7 = ((bf16[8,2,256,128]{3,2,1,0:T(8,128)(2,1)}), bf16[8,2,256,128]{3,2,1,0:T(8,128)(2,1)S(1)}, u32[]{:S(2)}, u32[]{:S(2)}) async-start(bf16[8,2,256,128]{3,2,1,0:T(8,128)(2,1)} %get-tuple-element.34), calls=%async_computation.7 | async-start | bytes 2097152 | tf_op jit(solution)/shard_map/all_to_all | solution.py:162
  305.4 29.5 %collective-permute-start.8 = (bf16[4,2,2,256,128]{4,3,2,1,0:T(8,128)(2,1)}, bf16[4,2,2,256,128]{4,3,2,1,0:T(8,128)(2,1)S(1)}, u32[]{:S(2)}, u32[]{:S(2)}) collective-permute-start(bf16[4,2,2,256,128]{4,3,2,1,0:T(8,128)(2,1)} %get-tuple-element.36), channel_id=1, source_target_pairs={{0,8},{8,16},{16,24},{1,9},{9,17},{17,25},{2,10},{10,18},{18,26},{... | collective-permute-start | bytes 3145736 | tf_op jit(solution)/shard_map/ppermute | solution.py:158
  307.3 46.1 %collective-permute-start.9 = (bf16[4,2,2,256,128]{4,3,2,1,0:T(8,128)(2,1)}, bf16[4,2,2,256,128]{4,3,2,1,0:T(8,128)(2,1)S(1)}, u32[]{:S(2)}, u32[]{:S(2)}) collective-permute-start(bf16[4,2,2,256,128]{4,3,2,1,0:T(8,128)(2,1)} %get-tuple-element.37), channel_id=1, source_target_pairs={{8,0},{16,8},{24,16},{9,1},{17,9},{25,17},{10,2},{18,10},{26,18},{... | collective-permute-start | bytes 3145736 | tf_op jit(solution)/shard_map/ppermute | solution.py:158
  358.2 56.6 %all-to-all-start.8 = ((bf16[8,2,2,256,128]{4,3,2,1,0:T(8,128)(2,1)}), bf16[8,2,2,256,128]{4,3,2,1,0:T(8,128)(2,1)S(1)}, u32[]{:S(2)}, u32[]{:S(2)}) async-start(bf16[8,2,2,256,128]{4,3,2,1,0:T(8,128)(2,1)} %add_convert_fusion.3), calls=%async_computation.8 | async-start | bytes 4194304 | tf_op jit(solution)/shard_map/all_to_all | solution.py:162
  364.8 46.1 %collective-permute-start.11 = (bf16[4,2,2,256,128]{4,3,2,1,0:T(8,128)(2,1)}, bf16[4,2,2,256,128]{4,3,2,1,0:T(8,128)(2,1)S(1)}, u32[]{:S(2)}, u32[]{:S(2)}) collective-permute-start(bf16[4,2,2,256,128]{4,3,2,1,0:T(8,128)(2,1)} %get-tuple-element.40), channel_id=1, source_target_pairs={{8,0},{16,8},{24,16},{9,1},{17,9},{25,17},{10,2},{18,10},{26,18},{... | collective-permute-start | bytes 3145736 | tf_op jit(solution)/shard_map/ppermute | solution.py:158
  414.8 56.6 %all-to-all-start.9 = ((bf16[8,2,2,256,128]{4,3,2,1,0:T(8,128)(2,1)}), bf16[8,2,2,256,128]{4,3,2,1,0:T(8,128)(2,1)}, u32[]{:S(2)}, u32[]{:S(2)}) async-start(bf16[8,2,2,256,128]{4,3,2,1,0:T(8,128)(2,1)} %add_convert_fusion.2), calls=%async_computation.9 | async-start | bytes 4194304 | tf_op jit(solution)/shard_map/all_to_all | solution.py:162
  421.4 46.1 %collective-permute-start.13 = (bf16[4,2,2,256,128]{4,3,2,1,0:T(8,128)(2,1)}, bf16[4,2,2,256,128]{4,3,2,1,0:T(8,128)(2,1)S(1)}, u32[]{:S(2)}, u32[]{:S(2)}) collective-permute-start(bf16[4,2,2,256,128]{4,3,2,1,0:T(8,128)(2,1)} %get-tuple-element.43), channel_id=1, source_target_pairs={{8,0},{16,8},{24,16},{9,1},{17,9},{25,17},{10,2},{18,10},{26,18},{... | collective-permute-start | bytes 3145736 | tf_op jit(solution)/shard_map/ppermute | solution.py:158
  471.4 56.7 %all-to-all-start.10 = ((bf16[8,2,2,256,128]{4,3,2,1,0:T(8,128)(2,1)}), bf16[8,2,2,256,128]{4,3,2,1,0:T(8,128)(2,1)}, u32[]{:S(2)}, u32[]{:S(2)}) async-start(bf16[8,2,2,256,128]{4,3,2,1,0:T(8,128)(2,1)} %add_convert_fusion.1), calls=%async_computation.10 | async-start | bytes 4194304 | tf_op jit(solution)/shard_map/all_to_all | solution.py:162
  478.1 46.1 %collective-permute-start.15 = (bf16[4,2,2,256,128]{4,3,2,1,0:T(8,128)(2,1)}, bf16[4,2,2,256,128]{4,3,2,1,0:T(8,128)(2,1)S(1)}, u32[]{:S(2)}, u32[]{:S(2)}) collective-permute-start(bf16[4,2,2,256,128]{4,3,2,1,0:T(8,128)(2,1)} %get-tuple-element.46), channel_id=1, source_target_pairs={{8,0},{16,8},{24,16},{9,1},{17,9},{25,17},{10,2},{18,10},{26,18},{... | collective-permute-start | bytes 3145736 | tf_op jit(solution)/shard_map/ppermute | solution.py:158
  528.1 53.9 %all-to-all-start.11 = ((bf16[8,2,2,256,128]{4,3,2,1,0:T(8,128)(2,1)}), bf16[8,2,2,256,128]{4,3,2,1,0:T(8,128)(2,1)}, u32[]{:S(2)}, u32[]{:S(2)}) async-start(bf16[8,2,2,256,128]{4,3,2,1,0:T(8,128)(2,1)} %add_convert_fusion), calls=%async_computation.11 | async-start | bytes 4194304 | tf_op jit(solution)/shard_map/all_to_all | solution.py:162
  (15 other events, 182.5 us)

commit v2 on v1

--- a/solution.py
+++ b/solution.py
@@ -101,13 +101,17 @@
 
 def attention(lists, key_counts, query_counts, q, o, g, low, own_low, own_high, high, first):
     heads, tokens, head_dim = q.shape
-    groups, here, piece, _ = g.shape
+    groups, _, piece, _ = g.shape
+    here = low.shape[1]
     half_groups = groups // 2
     step = 2 if here % 2 == 0 else 1
     half = tokens // 2
     nbr = lists.shape[0] // (tokens // TILE)
     rows = pl.BlockSpec((step, tokens, head_dim), lambda i, *_: (i + first // step, 0, 0))
     pieces = pl.BlockSpec((groups, step, piece, head_dim), lambda i, *_: (0, i, 0, 0))
+    g_pieces = pl.BlockSpec(
+        (groups, step, piece, head_dim), lambda i, *_: (0, i + first // step, 0, 0)
+    )
     halves = pl.BlockSpec((2, step, half, head_dim), lambda i, *_: (0, i, 0, 0))
 
     def outs(count):
@@ -128,7 +132,7 @@
         grid_spec=pltpu.PrefetchScalarGridSpec(
             num_scalar_prefetch=3,
             grid=(here // step,),
-            in_specs=[rows, rows, pieces, halves, halves, halves, halves],
+            in_specs=[rows, rows, g_pieces, halves, halves, halves, halves],
             out_specs=[pieces, outs(groups), outs(half_groups), outs(half_groups)],
             scratch_shapes=[
                 pltpu.VMEM((step, 2 * tokens, head_dim), jnp.bfloat16),
@@ -187,27 +191,39 @@
         ]
         return jnp.stack(cut)
 
+    kv = [(kv_half(c, 0), kv_half(c, half)) for c in range(chunks)]
+
+    def over_seq(rising, falling):
+        return shift(rising, True), shift(falling, False)
+
+    halos = [over_seq(kv[0][1], kv[0][0])]
+    out_grad = after(out_grad, kv[0])
+    grads = jnp.swapaxes(out_grad.reshape(seq_rows, groups, heads, head_dim), 0, 1)
+    grads = jnp.swapaxes(grads, 1, 2)
+    g = exchange(grads)
+    query_rows, attn_output = after((query_rows, attn_output), grads)
     q = jnp.swapaxes(query_rows, 0, 1)
     o = jnp.swapaxes(attn_output, 0, 1)
-    grads = jnp.swapaxes(out_grad.reshape(seq_rows, groups, heads, head_dim), 0, 1)
-    grads = jnp.swapaxes(grads, 1, 2)
-
-    dq_parts, dkv_parts = [], []
-    halo = None
+    for c in range(1, chunks):
+        own_low, own_high = after(kv[c], halos[-1])
+        halos.append(over_seq(own_high, own_low))
+
+    dq_parts, dk_parts, dv_parts = [], [], []
     for c in range(chunks):
-        own_low, own_high = kv_half(c, 0), kv_half(c, half)
-        send_low, send_high = after((own_low, own_high), halo)
-        low, high = shift(send_high, True), shift(send_low, False)
-        halo = (low, high)
-        g = exchange(grads[:, c * here : (c + 1) * here])
+        (low, high), (own_low, own_high) = halos[c], kv[c]
         dq, mid, flank_low, flank_high = attention(
             lists, key_counts, query_counts, q, o, g, low, own_low, own_high, high, c * here
         )
-        from_low, from_high = shift(flank_high, True), shift(flank_low, False)
         dq_parts.append(exchange(dq))
-        returned = jnp.concatenate([from_low, from_high], axis=0).astype(jnp.float32)
+        returned = jnp.concatenate(over_seq(flank_high, flank_low), axis=0).astype(jnp.float32)
         total = (mid.astype(jnp.float32) + returned).astype(jnp.bfloat16)
-        dkv_parts.append(exchange(total))
+        if c + 1 < chunks:
+            both = exchange(total)
+            dk_parts.append(both[:, 0])
+            dv_parts.append(both[:, 1])
+        else:
+            dk_parts.append(exchange(total[:, 0]))
+            dv_parts.append(exchange(after(total[:, 1], dk_parts[-1])))
 
     def finish(parts):
         whole = jnp.stack(parts, axis=1).reshape(groups * heads, seq_rows, head_dim)
@@ -215,8 +231,8 @@
 
     return (
         finish(dq_parts),
-        finish([part[:, 0] for part in dkv_parts]),
-        finish([part[:, 1] for part in dkv_parts]),
+        finish(dk_parts),
+        finish(dv_parts),
     )
 
 

time: 618 us -> 642 us (1.039)
  waiting for transfers between devices: 241 us -> 300 us
  blocking collectives: 31.4 us -> 0 us
    all_to_all x11 -> x10, waiting for transfers between devices: 44.4 us -> 87.7 us  [exchange(): lax.all_to_all(value, 'head', split_axis=0, concat_axis=0, tiled=True)]
    all_to_all x1 -> x0, blocking collectives: 31.4 us -> none  [exchange(): lax.all_to_all(value, 'head', split_axis=0, concat_axis=0, tiled=True)]
    ppermute x16, waiting for transfers between devices: 197 us -> 213 us  [shift(): return lax.ppermute(value, 'seq', pairs)]
    unnamed x26, local copies, waits for them, and re-layouts: 17.3 us -> 32.6 us
    optimization_barrier x0 -> x3, local copies, waits for them, and re-layouts: none -> 15.1 us  [after(): return lax.optimization_barrier((value, earlier))[0]]
    reshape x2 -> x0, local copies, waits for them, and re-layouts: 13.7 us -> none  [finish(): return jnp.swapaxes(whole, 0, 1).reshape(seq_rows, batch, width)]
    slice x5 -> x0, local copies, waits for them, and re-layouts: 13.4 us -> none  [the longest x4 9.42 us: per_device(): part[:, 1]]
    transpose x1 -> x0, local copies, waits for them, and re-layouts: 6.64 us -> none  [per_device(): o = jnp.swapaxes(attn_output, 0, 1)]
  transfers between devices with their start and end apart: 27 -> 26, of which waited for: 15 -> 15; matrix products, arithmetic and copies ran while one was open for 13% -> 9% of each run, Pallas kernels for 17% -> 16%
where the time goes in v2:
time: 642 us; the launch traced here: 634 us
  waiting for transfers between devices  300 us (47%)
  starting transfers between devices  103 us (16%)
  local copies, waits for them, and re-layouts  101 us (16%)
  Pallas kernels  101 us (16%)
  other arithmetic  28.3 us (4%)
    ppermute x16, waiting for transfers between devices, shift(): return lax.ppermute(value, 'seq', pairs)  213 us
    pallas_call x4, Pallas kernels, attention(): pl.pallas_call(functools.partial(attention_kernel, piece), out_shape=(mad...  101 us
    all_to_all x10, waiting for transfers between devices, exchange(): lax.all_to_all(value, 'head', split_axis=0, concat_axis=0, tiled=True)  87.7 us
    ppermute x16, starting transfers between devices, shift(): return lax.ppermute(value, 'seq', pairs)  56.8 us
    all_to_all x10, starting transfers between devices, exchange(): lax.all_to_all(value, 'head', split_axis=0, concat_axis=0, tiled=True)  45.9 us
    unnamed x26, local copies, waits for them, and re-layouts  32.6 us
    transpose x3, local copies, waits for them, and re-layouts, finish(): return jnp.swapaxes(whole, 0, 1).reshape(seq_rows, batch, width)  19.1 us
    optimization_barrier x3, local copies, waits for them, and re-layouts, after(): return lax.optimization_barrier((value, earlier))[0]  15.1 us
  transfers between devices with their start and end apart: 26, of which 15 were waited for; matrix products, arithmetic and copies ran while one was open for 9% of the time, Pallas kernels for 16%

profile of v2, /device:TPU:4, one launch (start us, length us, event | category | flops | bytes accessed | tf_op | source)
XLA Modules:
  0.0 634.3 jit_solution(6837892387904477441)
XLA Ops:
  0.6 10.3 %fusion = (bf16[1024,2,128]{2,1,0:T(2,128)(2,1)S(1)}, bf16[1024,2,128]{2,1,0:T(2,128)(2,1)S(1)}, bf16[1024,2,128]{2,1,0:T(2,128)(2,1)S(1)}, bf16[1024,2,128]{2,1...) fusion(bf16[2048,8,128]{2,1,0:T(8,128)(2,1)} %param.8), kind=kLoop, calls=%fused_computation.43 | loop fusion | bytes 8388608 | tf_op jit(solution)/shard_map/slice | solution.py:189
  17.7 7.5 %copy.118 = bf16[256,4,2048]{0,2,1:T(8,128)(2,1)} copy(bf16[256,4,2048]{2,1,0:T(4,128)(2,1)} %param.11) | data formatting | bytes 8388608 | tf_op jit(solution)/shard_map/optimization_barrier | solution.py:156
  25.2 6.4 %copy.119 = bf16[256,8,8,128]{3,0,2,1:T(8,128)(2,1)} copy(bf16[256,8,8,128]{0,3,2,1:T(8,128)(2,1)} %bitcast.113) | data formatting | bytes 8388608 | tf_op jit(solution)/shard_map/reshape | solution.py:201
  54.9 10.6 %collective-permute-done.low_ref = bf16[2,2,1024,128]{3,2,1,0:T(8,128)(2,1)} collective-permute-done((bf16[2,2,1024,128]{3,2,1,0:T(8,128)(2,1)}, bf16[2,2,1024,128]{3,2,1,0:T(8,128)(2,1)}, u32[]{:S(2)}, u32[]{:S(2)}) %collective-permute-start) | collective-permute-done | bytes 1048608 | tf_op jit(solution)/shard_map/ppermute | solution.py:162
  65.5 20.2 %collective-permute-done.1.high_ref = bf16[2,2,1024,128]{3,2,1,0:T(8,128)(2,1)} collective-permute-done((bf16[2,2,1024,128]{3,2,1,0:T(8,128)(2,1)}, bf16[2,2,1024,128]{3,2,1,0:T(8,128)(2,1)}, u32[]{:S(2)}, u32[]{:S(2)}) %collective-permute-start.1) | collective-permute-done | bytes 1048608 | tf_op jit(solution)/shard_map/ppermute | solution.py:162
  92.9 37.6 %all-to-all-done.g_ref = bf16[8,8,256,128]{3,2,1,0:T(8,128)(2,1)} async-done(((bf16[8,8,256,128]{3,2,1,0:T(8,128)(2,1)}), bf16[8,8,256,128]{3,2,1,0:T(8,128)(2,1)}, u32[]{:S(2)}, u32[]{:S(2)}) %all-to-all-start) | async-done | bytes 4194336 | tf_op jit(solution)/shard_map/all_to_all | solution.py:166
  130.6 25.2 %shard_map.94 = (bf16[8,2,256,128]{3,2,1,0:T(8,128)(2,1)}, bf16[8,2,2,256,128]{4,3,2,1,0:T(8,128)(2,1)}, bf16[4,2,2,256,128]{4,3,2,1,0:T(8,128)(2,1)}, bf16[4,2,2,256,128]{4,3,2,1,0:T(8,128)(2,1)}) custom-call(s32[64]{0:T(128)S(1)} %reshape.30.lists, s32[32]{0:T(128)S(1)} %pad_dynamic-slice_fusion.key_counts, s32[16]{0:T(128)S(1)} %dynamic_slice.11.query_counts, ...), custom_call_target="tpu_custom_call" | custom-call | flops 10737418240 | bytes 12582912 | tf_op jit(solution)/shard_map/pallas_call | solution.py:124
  169.9 25.3 %shard_map.95 = (bf16[8,2,256,128]{3,2,1,0:T(8,128)(2,1)}, bf16[8,2,2,256,128]{4,3,2,1,0:T(8,128)(2,1)}, bf16[4,2,2,256,128]{4,3,2,1,0:T(8,128)(2,1)}, bf16[4,2,2,256,128]{4,3,2,1,0:T(8,128)(2,1)}) custom-call(s32[64]{0:T(128)S(1)} %reshape.30.lists, s32[32]{0:T(128)S(1)} %pad_dynamic-slice_fusion.key_counts, s32[16]{0:T(128)S(1)} %dynamic_slice.11.query_counts, ...), custom_call_target="tpu_custom_call" | custom-call | flops 10737418240 | bytes 12582912 | tf_op jit(solution)/shard_map/pallas_call | solution.py:124
  203.8 8.3 %collective-permute-done.5.high_ref = bf16[2,2,1024,128]{3,2,1,0:T(8,128)(2,1)} collective-permute-done((bf16[2,2,1024,128]{3,2,1,0:T(8,128)(2,1)}, bf16[2,2,1024,128]{3,2,1,0:T(8,128)(2,1)}, u32[]{:S(2)}, u32[]{:S(2)}) %collective-permute-start.5) | collective-permute-done | bytes 1048608 | tf_op jit(solution)/shard_map/ppermute | solution.py:162
  219.4 25.1 %shard_map.96 = (bf16[8,2,256,128]{3,2,1,0:T(8,128)(2,1)}, bf16[8,2,2,256,128]{4,3,2,1,0:T(8,128)(2,1)}, bf16[4,2,2,256,128]{4,3,2,1,0:T(8,128)(2,1)}, bf16[4,2,2,256,128]{4,3,2,1,0:T(8,128)(2,1)}) custom-call(s32[64]{0:T(128)S(1)} %reshape.30.lists, s32[32]{0:T(128)S(1)} %pad_dynamic-slice_fusion.key_counts, s32[16]{0:T(128)S(1)} %dynamic_slice.11.query_counts, ...), custom_call_target="tpu_custom_call" | custom-call | flops 10737418240 | bytes 12582912 | tf_op jit(solution)/shard_map/pallas_call | solution.py:124
  249.2 10.1 %collective-permute-done.7.high_ref = bf16[2,2,1024,128]{3,2,1,0:T(8,128)(2,1)} collective-permute-done((bf16[2,2,1024,128]{3,2,1,0:T(8,128)(2,1)}, bf16[2,2,1024,128]{3,2,1,0:T(8,128)(2,1)}, u32[]{:S(2)}, u32[]{:S(2)}) %collective-permute-start.7) | collective-permute-done | bytes 1048608 | tf_op jit(solution)/shard_map/ppermute | solution.py:162
  259.3 25.2 %shard_map.97 = (bf16[8,2,256,128]{3,2,1,0:T(8,128)(2,1)}, bf16[8,2,2,256,128]{4,3,2,1,0:T(8,128)(2,1)}, bf16[4,2,2,256,128]{4,3,2,1,0:T(8,128)(2,1)}, bf16[4,2,2,256,128]{4,3,2,1,0:T(8,128)(2,1)}) custom-call(s32[64]{0:T(128)S(1)} %reshape.30.lists, s32[32]{0:T(128)S(1)} %pad_dynamic-slice_fusion.key_counts, s32[16]{0:T(128)S(1)} %dynamic_slice.11.query_counts, ...), custom_call_target="tpu_custom_call" | custom-call | flops 10737418240 | bytes 12582912 | tf_op jit(solution)/shard_map/pallas_call | solution.py:124
  296.2 22.3 %collective-permute-done.14 = bf16[4,2,2,256,128]{4,3,2,1,0:T(8,128)(2,1)S(1)} collective-permute-done((bf16[4,2,2,256,128]{4,3,2,1,0:T(8,128)(2,1)}, bf16[4,2,2,256,128]{4,3,2,1,0:T(8,128)(2,1)S(1)}, u32[]{:S(2)}, u32[]{:S(2)}) %collective-permute-start.14) | collective-permute-done | bytes 1048608 | tf_op jit(solution)/shard_map/ppermute | solution.py:162
  318.5 18.6 %collective-permute-done.15 = bf16[4,2,2,256,128]{4,3,2,1,0:T(8,128)(2,1)S(1)} collective-permute-done((bf16[4,2,2,256,128]{4,3,2,1,0:T(8,128)(2,1)}, bf16[4,2,2,256,128]{4,3,2,1,0:T(8,128)(2,1)S(1)}, u32[]{:S(2)}, u32[]{:S(2)}) %collective-permute-start.15) | collective-permute-done | bytes 1048608 | tf_op jit(solution)/shard_map/ppermute | solution.py:162
  354.0 22.3 %collective-permute-done.8 = bf16[4,2,2,256,128]{4,3,2,1,0:T(8,128)(2,1)S(1)} collective-permute-done((bf16[4,2,2,256,128]{4,3,2,1,0:T(8,128)(2,1)}, bf16[4,2,2,256,128]{4,3,2,1,0:T(8,128)(2,1)S(1)}, u32[]{:S(2)}, u32[]{:S(2)}) %collective-permute-start.8) | collective-permute-done | bytes 1048608 | tf_op jit(solution)/shard_map/ppermute | solution.py:162
  376.3 18.6 %collective-permute-done.9 = bf16[4,2,2,256,128]{4,3,2,1,0:T(8,128)(2,1)S(1)} collective-permute-done((bf16[4,2,2,256,128]{4,3,2,1,0:T(8,128)(2,1)}, bf16[4,2,2,256,128]{4,3,2,1,0:T(8,128)(2,1)S(1)}, u32[]{:S(2)}, u32[]{:S(2)}) %collective-permute-start.9) | collective-permute-done | bytes 1048608 | tf_op jit(solution)/shard_map/ppermute | solution.py:162
  411.5 22.3 %collective-permute-done.10 = bf16[4,2,2,256,128]{4,3,2,1,0:T(8,128)(2,1)S(1)} collective-permute-done((bf16[4,2,2,256,128]{4,3,2,1,0:T(8,128)(2,1)}, bf16[4,2,2,256,128]{4,3,2,1,0:T(8,128)(2,1)S(1)}, u32[]{:S(2)}, u32[]{:S(2)}) %collective-permute-start.10) | collective-permute-done | bytes 1048608 | tf_op jit(solution)/shard_map/ppermute | solution.py:162
  433.8 18.6 %collective-permute-done.11 = bf16[4,2,2,256,128]{4,3,2,1,0:T(8,128)(2,1)S(1)} collective-permute-done((bf16[4,2,2,256,128]{4,3,2,1,0:T(8,128)(2,1)}, bf16[4,2,2,256,128]{4,3,2,1,0:T(8,128)(2,1)S(1)}, u32[]{:S(2)}, u32[]{:S(2)}) %collective-permute-start.11) | collective-permute-done | bytes 1048608 | tf_op jit(solution)/shard_map/ppermute | solution.py:162
  468.1 22.3 %collective-permute-done.12 = bf16[4,2,2,256,128]{4,3,2,1,0:T(8,128)(2,1)S(1)} collective-permute-done((bf16[4,2,2,256,128]{4,3,2,1,0:T(8,128)(2,1)}, bf16[4,2,2,256,128]{4,3,2,1,0:T(8,128)(2,1)S(1)}, u32[]{:S(2)}, u32[]{:S(2)}) %collective-permute-start.12) | collective-permute-done | bytes 1048608 | tf_op jit(solution)/shard_map/ppermute | solution.py:162
  490.4 18.6 %collective-permute-done.13 = bf16[4,2,2,256,128]{4,3,2,1,0:T(8,128)(2,1)S(1)} collective-permute-done((bf16[4,2,2,256,128]{4,3,2,1,0:T(8,128)(2,1)}, bf16[4,2,2,256,128]{4,3,2,1,0:T(8,128)(2,1)S(1)}, u32[]{:S(2)}, u32[]{:S(2)}) %collective-permute-start.13) | collective-permute-done | bytes 1048608 | tf_op jit(solution)/shard_map/ppermute | solution.py:162
  517.5 49.2 %all-to-all-done.7 = bf16[8,2,2,256,128]{4,3,2,1,0:T(8,128)(2,1)} async-done(((bf16[8,2,2,256,128]{4,3,2,1,0:T(8,128)(2,1)}), bf16[8,2,2,256,128]{4,3,2,1,0:T(8,128)(2,1)}, u32[]{:S(2)}, u32[]{:S(2)}) %all-to-all-start.7) | async-done | bytes 2097184 | tf_op jit(solution)/shard_map/all_to_all | solution.py:166
  581.7 7.8 %copy.146 = bf16[256,4,2048]{2,1,0:T(4,128)(2,1)} copy(bf16[256,4,2048]{0,2,1:T(8,128)(2,1)} %bitcast.108) | data formatting | bytes 8388608
  608.3 7.9 %copy.148 = bf16[256,4,2048]{2,1,0:T(4,128)(2,1)} copy(bf16[256,4,2048]{0,2,1:T(8,128)(2,1)} %bitcast.110) | data formatting | bytes 8388608
  626.5 7.8 %copy.147 = bf16[256,4,2048]{2,1,0:T(4,128)(2,1)} copy(bf16[256,4,2048]{0,2,1:T(8,128)(2,1)} %bitcast.112) | data formatting | bytes 8388608
  (99 shorter events, 185.4 us)
Async XLA Ops:
  31.6 99.0 %all-to-all-start = ((bf16[8,8,256,128]{3,2,1,0:T(8,128)(2,1)}), bf16[8,8,256,128]{3,2,1,0:T(8,128)(2,1)}, u32[]{:S(2)}, u32[]{:S(2)}) async-start(bf16[8,8,256,128]{3,2,1,0:T(8,128)(2,1)} %bitcast.106), calls=%async_computation | async-start | bytes 8388608 | tf_op jit(solution)/shard_map/all_to_all | solution.py:166
  39.9 45.9 %collective-permute-start.1 = (bf16[2,2,1024,128]{3,2,1,0:T(8,128)(2,1)}, bf16[2,2,1024,128]{3,2,1,0:T(8,128)(2,1)}, u32[]{:S(2)}, u32[]{:S(2)}) collective-permute-start(bf16[2,2,1024,128]{3,2,1,0:T(8,128)(2,1)} %pad_maximum_fusion.3.own_low_ref), channel_id=1, source_target_pairs={{8,0},{16,8},{24,16},{9,1},{17,9},{25,17},{10,2},{18,10},{26,18},{... | collective-permute-start | bytes 3145736 | tf_op jit(solution)/shard_map/ppermute | solution.py:162
  85.7 77.2 %collective-permute-start.2 = (bf16[2,2,1024,128]{3,2,1,0:T(8,128)(2,1)}, bf16[2,2,1024,128]{3,2,1,0:T(8,128)(2,1)}, u32[]{:S(2)}, u32[]{:S(2)}) collective-permute-start(bf16[2,2,1024,128]{3,2,1,0:T(8,128)(2,1)} %pad_maximum_fusion.6.own_high_ref), channel_id=1, source_target_pairs={{0,8},{8,16},{16,24},{1,9},{9,17},{17,25},{2,10},{10,18},{18,26},{... | collective-permute-start | bytes 3145736 | tf_op jit(solution)/shard_map/ppermute | solution.py:162
  87.6 75.3 %collective-permute-start.3 = (bf16[2,2,1024,128]{3,2,1,0:T(8,128)(2,1)}, bf16[2,2,1024,128]{3,2,1,0:T(8,128)(2,1)}, u32[]{:S(2)}, u32[]{:S(2)}) collective-permute-start(bf16[2,2,1024,128]{3,2,1,0:T(8,128)(2,1)} %pad_maximum_fusion.5.own_low_ref), channel_id=1, source_target_pairs={{8,0},{16,8},{24,16},{9,1},{17,9},{25,17},{10,2},{18,10},{26,18},{... | collective-permute-start | bytes 3145736 | tf_op jit(solution)/shard_map/ppermute | solution.py:162
  155.8 39.4 %all-to-all-start.1 = ((bf16[8,2,256,128]{3,2,1,0:T(8,128)(2,1)}), bf16[8,2,256,128]{3,2,1,0:T(8,128)(2,1)S(1)}, u32[]{:S(2)}, u32[]{:S(2)}) async-start(bf16[8,2,256,128]{3,2,1,0:T(8,128)(2,1)} %get-tuple-element.32), calls=%async_computation.1 | async-start | bytes 2097152 | tf_op jit(solution)/shard_map/all_to_all | solution.py:166
  163.0 40.9 %collective-permute-start.4 = (bf16[2,2,1024,128]{3,2,1,0:T(8,128)(2,1)}, bf16[2,2,1024,128]{3,2,1,0:T(8,128)(2,1)}, u32[]{:S(2)}, u32[]{:S(2)}) collective-permute-start(bf16[2,2,1024,128]{3,2,1,0:T(8,128)(2,1)} %pad_maximum_fusion.8.own_high_ref), channel_id=1, source_target_pairs={{0,8},{8,16},{16,24},{1,9},{9,17},{17,25},{2,10},{10,18},{18,26},{... | collective-permute-start | bytes 3145736 | tf_op jit(solution)/shard_map/ppermute | solution.py:162
  166.4 45.8 %collective-permute-start.5 = (bf16[2,2,1024,128]{3,2,1,0:T(8,128)(2,1)}, bf16[2,2,1024,128]{3,2,1,0:T(8,128)(2,1)}, u32[]{:S(2)}, u32[]{:S(2)}) collective-permute-start(bf16[2,2,1024,128]{3,2,1,0:T(8,128)(2,1)} %pad_maximum_fusion.7.own_low_ref), channel_id=1, source_target_pairs={{8,0},{16,8},{24,16},{9,1},{17,9},{25,17},{10,2},{18,10},{26,18},{... | collective-permute-start | bytes 3145736 | tf_op jit(solution)/shard_map/ppermute | solution.py:162
  195.2 49.3 %all-to-all-start.2 = ((bf16[8,2,256,128]{3,2,1,0:T(8,128)(2,1)}), bf16[8,2,256,128]{3,2,1,0:T(8,128)(2,1)S(1)}, u32[]{:S(2)}, u32[]{:S(2)}) async-start(bf16[8,2,256,128]{3,2,1,0:T(8,128)(2,1)} %get-tuple-element.35), calls=%async_computation.2 | async-start | bytes 2097152 | tf_op jit(solution)/shard_map/all_to_all | solution.py:166
  212.1 37.1 %collective-permute-start.6 = (bf16[2,2,1024,128]{3,2,1,0:T(8,128)(2,1)}, bf16[2,2,1024,128]{3,2,1,0:T(8,128)(2,1)}, u32[]{:S(2)}, u32[]{:S(2)}) collective-permute-start(bf16[2,2,1024,128]{3,2,1,0:T(8,128)(2,1)} %pad_maximum_fusion.10.own_high_ref), channel_id=1, source_target_pairs={{0,8},{8,16},{16,24},{1,9},{9,17},{17,25},{2,10},{10,18},{18,26},{... | collective-permute-start | bytes 3145736 | tf_op jit(solution)/shard_map/ppermute | solution.py:162
  214.1 45.3 %collective-permute-start.7 = (bf16[2,2,1024,128]{3,2,1,0:T(8,128)(2,1)}, bf16[2,2,1024,128]{3,2,1,0:T(8,128)(2,1)}, u32[]{:S(2)}, u32[]{:S(2)}) collective-permute-start(bf16[2,2,1024,128]{3,2,1,0:T(8,128)(2,1)} %pad_maximum_fusion.9.own_low_ref), channel_id=1, source_target_pairs={{8,0},{16,8},{24,16},{9,1},{17,9},{25,17},{10,2},{18,10},{26,18},{... | collective-permute-start | bytes 3145736 | tf_op jit(solution)/shard_map/ppermute | solution.py:162
  244.5 40.1 %all-to-all-start.3 = ((bf16[8,2,256,128]{3,2,1,0:T(8,128)(2,1)}), bf16[8,2,256,128]{3,2,1,0:T(8,128)(2,1)S(1)}, u32[]{:S(2)}, u32[]{:S(2)}) async-start(bf16[8,2,256,128]{3,2,1,0:T(8,128)(2,1)} %get-tuple-element.38), calls=%async_computation.3 | async-start | bytes 2097152 | tf_op jit(solution)/shard_map/all_to_all | solution.py:166
  284.6 56.5 %all-to-all-start.4 = ((bf16[8,2,256,128]{3,2,1,0:T(8,128)(2,1)}), bf16[8,2,256,128]{3,2,1,0:T(8,128)(2,1)S(1)}, u32[]{:S(2)}, u32[]{:S(2)}) async-start(bf16[8,2,256,128]{3,2,1,0:T(8,128)(2,1)} %get-tuple-element.41), calls=%async_computation.4 | async-start | bytes 2097152 | tf_op jit(solution)/shard_map/all_to_all | solution.py:166
  289.0 29.5 %collective-permute-start.14 = (bf16[4,2,2,256,128]{4,3,2,1,0:T(8,128)(2,1)}, bf16[4,2,2,256,128]{4,3,2,1,0:T(8,128)(2,1)S(1)}, u32[]{:S(2)}, u32[]{:S(2)}) collective-permute-start(bf16[4,2,2,256,128]{4,3,2,1,0:T(8,128)(2,1)} %get-tuple-element.52), channel_id=1, source_target_pairs={{0,8},{8,16},{16,24},{1,9},{9,17},{17,25},{2,10},{10,18},{18,26},{... | collective-permute-start | bytes 3145736 | tf_op jit(solution)/shard_map/ppermute | solution.py:162
  290.9 46.1 %collective-permute-start.15 = (bf16[4,2,2,256,128]{4,3,2,1,0:T(8,128)(2,1)}, bf16[4,2,2,256,128]{4,3,2,1,0:T(8,128)(2,1)S(1)}, u32[]{:S(2)}, u32[]{:S(2)}) collective-permute-start(bf16[4,2,2,256,128]{4,3,2,1,0:T(8,128)(2,1)} %get-tuple-element.53), channel_id=1, source_target_pairs={{8,0},{16,8},{24,16},{9,1},{17,9},{25,17},{10,2},{18,10},{26,18},{... | collective-permute-start | bytes 3145736 | tf_op jit(solution)/shard_map/ppermute | solution.py:162
  342.1 56.5 %all-to-all-start.8 = ((bf16[8,2,256,128]{3,2,1,0:T(8,128)(2,1)}), bf16[8,2,256,128]{3,2,1,0:T(8,128)(2,1)S(1)}, u32[]{:S(2)}, u32[]{:S(2)}) async-start(bf16[8,2,256,128]{3,2,1,0:T(8,128)(2,1)} %get-tuple-element.84), calls=%async_computation.8 | async-start | bytes 2097152 | tf_op jit(solution)/shard_map/all_to_all | solution.py:166
  346.8 29.5 %collective-permute-start.8 = (bf16[4,2,2,256,128]{4,3,2,1,0:T(8,128)(2,1)}, bf16[4,2,2,256,128]{4,3,2,1,0:T(8,128)(2,1)S(1)}, u32[]{:S(2)}, u32[]{:S(2)}) collective-permute-start(bf16[4,2,2,256,128]{4,3,2,1,0:T(8,128)(2,1)} %get-tuple-element.43), channel_id=1, source_target_pairs={{0,8},{8,16},{16,24},{1,9},{9,17},{17,25},{2,10},{10,18},{18,26},{... | collective-permute-start | bytes 3145736 | tf_op jit(solution)/shard_map/ppermute | solution.py:162
  348.7 46.1 %collective-permute-start.9 = (bf16[4,2,2,256,128]{4,3,2,1,0:T(8,128)(2,1)}, bf16[4,2,2,256,128]{4,3,2,1,0:T(8,128)(2,1)S(1)}, u32[]{:S(2)}, u32[]{:S(2)}) collective-permute-start(bf16[4,2,2,256,128]{4,3,2,1,0:T(8,128)(2,1)} %get-tuple-element.44), channel_id=1, source_target_pairs={{8,0},{16,8},{24,16},{9,1},{17,9},{25,17},{10,2},{18,10},{26,18},{... | collective-permute-start | bytes 3145736 | tf_op jit(solution)/shard_map/ppermute | solution.py:162
  399.6 56.6 %all-to-all-start.5 = ((bf16[8,2,2,256,128]{4,3,2,1,0:T(8,128)(2,1)}), bf16[8,2,2,256,128]{4,3,2,1,0:T(8,128)(2,1)S(1)}, u32[]{:S(2)}, u32[]{:S(2)}) async-start(bf16[8,2,2,256,128]{4,3,2,1,0:T(8,128)(2,1)} %add_convert_fusion.3), calls=%async_computation.5 | async-start | bytes 4194304 | tf_op jit(solution)/shard_map/all_to_all | solution.py:166
  404.3 29.5 %collective-permute-start.10 = (bf16[4,2,2,256,128]{4,3,2,1,0:T(8,128)(2,1)}, bf16[4,2,2,256,128]{4,3,2,1,0:T(8,128)(2,1)S(1)}, u32[]{:S(2)}, u32[]{:S(2)}) collective-permute-start(bf16[4,2,2,256,128]{4,3,2,1,0:T(8,128)(2,1)} %get-tuple-element.46), channel_id=1, source_target_pairs={{0,8},{8,16},{16,24},{1,9},{9,17},{17,25},{2,10},{10,18},{18,26},{... | collective-permute-start | bytes 3145736 | tf_op jit(solution)/shard_map/ppermute | solution.py:162
  406.2 46.1 %collective-permute-start.11 = (bf16[4,2,2,256,128]{4,3,2,1,0:T(8,128)(2,1)}, bf16[4,2,2,256,128]{4,3,2,1,0:T(8,128)(2,1)S(1)}, u32[]{:S(2)}, u32[]{:S(2)}) collective-permute-start(bf16[4,2,2,256,128]{4,3,2,1,0:T(8,128)(2,1)} %get-tuple-element.47), channel_id=1, source_target_pairs={{8,0},{16,8},{24,16},{9,1},{17,9},{25,17},{10,2},{18,10},{26,18},{... | collective-permute-start | bytes 3145736 | tf_op jit(solution)/shard_map/ppermute | solution.py:162
  456.2 56.6 %all-to-all-start.6 = ((bf16[8,2,2,256,128]{4,3,2,1,0:T(8,128)(2,1)}), bf16[8,2,2,256,128]{4,3,2,1,0:T(8,128)(2,1)}, u32[]{:S(2)}, u32[]{:S(2)}) async-start(bf16[8,2,2,256,128]{4,3,2,1,0:T(8,128)(2,1)} %add_convert_fusion.2), calls=%async_computation.6 | async-start | bytes 4194304 | tf_op jit(solution)/shard_map/all_to_all | solution.py:166
  462.8 46.1 %collective-permute-start.13 = (bf16[4,2,2,256,128]{4,3,2,1,0:T(8,128)(2,1)}, bf16[4,2,2,256,128]{4,3,2,1,0:T(8,128)(2,1)S(1)}, u32[]{:S(2)}, u32[]{:S(2)}) collective-permute-start(bf16[4,2,2,256,128]{4,3,2,1,0:T(8,128)(2,1)} %get-tuple-element.50), channel_id=1, source_target_pairs={{8,0},{16,8},{24,16},{9,1},{17,9},{25,17},{10,2},{18,10},{26,18},{... | collective-permute-start | bytes 3145736 | tf_op jit(solution)/shard_map/ppermute | solution.py:162
  512.7 53.9 %all-to-all-start.7 = ((bf16[8,2,2,256,128]{4,3,2,1,0:T(8,128)(2,1)}), bf16[8,2,2,256,128]{4,3,2,1,0:T(8,128)(2,1)}, u32[]{:S(2)}, u32[]{:S(2)}) async-start(bf16[8,2,2,256,128]{4,3,2,1,0:T(8,128)(2,1)} %add_convert_fusion.1), calls=%async_computation.7 | async-start | bytes 4194304 | tf_op jit(solution)/shard_map/all_to_all | solution.py:166
  566.7 30.8 %all-to-all-start.9 = ((bf16[8,2,256,128]{3,2,1,0:T(8,128)(2,1)}), bf16[8,2,256,128]{3,2,1,0:T(8,128)(2,1)}, u32[]{:S(2)}, u32[]{:S(2)}) async-start(bf16[8,2,256,128]{3,2,1,0:T(8,128)(2,1)} %get-tuple-element.54), calls=%async_computation.9 | async-start | bytes 2097152 | tf_op jit(solution)/shard_map/all_to_all | solution.py:166
  (12 other events, 191.2 us)

commit v3 on v2

--- a/solution.py
+++ b/solution.py
@@ -208,32 +208,37 @@
         own_low, own_high = after(kv[c], halos[-1])
         halos.append(over_seq(own_high, own_low))
 
-    dq_parts, dk_parts, dv_parts = [], [], []
+    def finish(parts):
+        whole = jnp.stack(parts, axis=1).reshape(groups * heads, seq_rows, head_dim)
+        return jnp.swapaxes(whole, 0, 1).reshape(seq_rows, batch, width)
+
+    dq_parts, dk_parts, dv_parts, made = [], [], [], []
     for c in range(chunks):
         (low, high), (own_low, own_high) = halos[c], kv[c]
-        dq, mid, flank_low, flank_high = attention(
+        dq, *rest = attention(
             lists, key_counts, query_counts, q, o, g, low, own_low, own_high, high, c * here
         )
         dq_parts.append(exchange(dq))
-        returned = jnp.concatenate(over_seq(flank_high, flank_low), axis=0).astype(jnp.float32)
+        made.append(rest)
+    grad_query = finish(dq_parts)
+    earlier, total = halos[-1], None
+    for c, (mid, flank_low, flank_high) in enumerate(made):
+        last = c + 1 == chunks
+        if last:
+            earlier = (earlier, grad_query, total) if c else grad_query
+        earlier = over_seq(*after((flank_high, flank_low), earlier))
+        returned = jnp.concatenate(earlier, axis=0).astype(jnp.float32)
         total = (mid.astype(jnp.float32) + returned).astype(jnp.bfloat16)
-        if c + 1 < chunks:
+        if last:
+            total = after(total, dk_parts[-1] if c else None)
+            dk_parts.append(exchange(total[:, 0]))
+            grad_key = finish(dk_parts)
+            dv_parts.append(exchange(after(total[:, 1], dk_parts[-1])))
+        else:
             both = exchange(total)
             dk_parts.append(both[:, 0])
             dv_parts.append(both[:, 1])
-        else:
-            dk_parts.append(exchange(total[:, 0]))
-            dv_parts.append(exchange(after(total[:, 1], dk_parts[-1])))
-
-    def finish(parts):
-        whole = jnp.stack(parts, axis=1).reshape(groups * heads, seq_rows, head_dim)
-        return jnp.swapaxes(whole, 0, 1).reshape(seq_rows, batch, width)
-
-    return (
-        finish(dq_parts),
-        finish(dk_parts),
-        finish(dv_parts),
-    )
+    return grad_query, grad_key, finish(dv_parts)
 
 
 def solution(mesh):

time: 642 us -> 684 us (1.065)
  blocking collectives: 0 us -> 30.9 us
  waiting for transfers between devices: 300 us -> 325 us
    ppermute x16, waiting for transfers between devices: 213 us -> 275 us  [shift(): return lax.ppermute(value, 'seq', pairs)]
    all_to_all x10 -> x9, waiting for transfers between devices: 87.7 us -> 50.5 us  [exchange(): lax.all_to_all(value, 'head', split_axis=0, concat_axis=0, tiled=True)]
    all_to_all x0 -> x1, blocking collectives: none -> 30.9 us  [exchange(): lax.all_to_all(value, 'head', split_axis=0, concat_axis=0, tiled=True)]
    all_to_all x10 -> x9, starting transfers between devices: 45.9 us -> 39.8 us  [exchange(): lax.all_to_all(value, 'head', split_axis=0, concat_axis=0, tiled=True)]
    unnamed x26 -> x44, local copies, waits for them, and re-layouts: 32.6 us -> 30.3 us
  transfers between devices with their start and end apart: 26 -> 25, of which waited for: 15 -> 17; matrix products, arithmetic and copies ran while one was open for 9% -> 11% of each run, Pallas kernels for 16% -> 11%
where the time goes in v3:
time: 684 us; the launch traced here: 676 us
  waiting for transfers between devices  325 us (48%)
  Pallas kernels  101 us (15%)
  local copies, waits for them, and re-layouts  99.9 us (15%)
  starting transfers between devices  96.3 us (14%)
  blocking collectives  30.9 us (5%)
  other arithmetic  22 us (3%)
    ppermute x16, waiting for transfers between devices, shift(): return lax.ppermute(value, 'seq', pairs)  275 us
    pallas_call x4, Pallas kernels, attention(): pl.pallas_call(functools.partial(attention_kernel, piece), out_shape=(mad...  101 us
    ppermute x16, starting transfers between devices, shift(): return lax.ppermute(value, 'seq', pairs)  56.5 us
    all_to_all x9, waiting for transfers between devices, exchange(): lax.all_to_all(value, 'head', split_axis=0, concat_axis=0, tiled=True)  50.5 us
    all_to_all x9, starting transfers between devices, exchange(): lax.all_to_all(value, 'head', split_axis=0, concat_axis=0, tiled=True)  39.8 us
    all_to_all x1, blocking collectives, exchange(): lax.all_to_all(value, 'head', split_axis=0, concat_axis=0, tiled=True)  30.9 us
    unnamed x44, local copies, waits for them, and re-layouts  30.3 us
    transpose x3, local copies, waits for them, and re-layouts, finish(): return jnp.swapaxes(whole, 0, 1).reshape(seq_rows, batch, width)  19.1 us
  transfers between devices with their start and end apart: 25, of which 17 were waited for; matrix products, arithmetic and copies ran while one was open for 11% of the time, Pallas kernels for 11%

profile of v3, /device:TPU:4, one launch (start us, length us, event | category | flops | bytes accessed | tf_op | source)
XLA Modules:
  0.0 676.4 jit_solution(2722731712320578701)
XLA Ops:
  0.6 11.1 %fusion = (bf16[1024,2,128]{2,1,0:T(2,128)(2,1)S(1)}, bf16[1024,2,128]{2,1,0:T(2,128)(2,1)S(1)}, bf16[1024,2,128]{2,1,0:T(2,128)(2,1)S(1)}, bf16[1024,2,128]{2,1...) fusion(bf16[2048,8,128]{2,1,0:T(8,128)(2,1)} %param.8), kind=kLoop, calls=%fused_computation.43 | loop fusion | bytes 8388608 | tf_op jit(solution)/shard_map/slice | solution.py:189
  45.6 19.0 %collective-permute-done.1.high_ref = bf16[2,2,1024,128]{3,2,1,0:T(8,128)(2,1)S(1)} collective-permute-done((bf16[2,2,1024,128]{3,2,1,0:T(8,128)(2,1)}, bf16[2,2,1024,128]{3,2,1,0:T(8,128)(2,1)S(1)}, u32[]{:S(2)}, u32[]{:S(2)}) %collective-permute-start.1) | collective-permute-done | bytes 1048608 | tf_op jit(solution)/shard_map/ppermute | solution.py:162
  64.6 22.4 %collective-permute-done.low_ref = bf16[2,2,1024,128]{3,2,1,0:T(8,128)(2,1)S(1)} collective-permute-done((bf16[2,2,1024,128]{3,2,1,0:T(8,128)(2,1)}, bf16[2,2,1024,128]{3,2,1,0:T(8,128)(2,1)S(1)}, u32[]{:S(2)}, u32[]{:S(2)}) %collective-permute-start) | collective-permute-done | bytes 1048608 | tf_op jit(solution)/shard_map/ppermute | solution.py:162
  94.3 21.5 %collective-permute-done.2.low_ref = bf16[2,2,1024,128]{3,2,1,0:T(8,128)(2,1)S(1)} collective-permute-done((bf16[2,2,1024,128]{3,2,1,0:T(8,128)(2,1)S(1)}, bf16[2,2,1024,128]{3,2,1,0:T(8,128)(2,1)S(1)}, u32[]{:S(2)}, u32[]{:S(2)}) %collective-permute-start.2) | collective-permute-done | bytes 1048608 | tf_op jit(solution)/shard_map/ppermute | solution.py:162
  115.8 19.4 %collective-permute-done.3.high_ref = bf16[2,2,1024,128]{3,2,1,0:T(8,128)(2,1)S(1)} collective-permute-done((bf16[2,2,1024,128]{3,2,1,0:T(8,128)(2,1)S(1)}, bf16[2,2,1024,128]{3,2,1,0:T(8,128)(2,1)S(1)}, u32[]{:S(2)}, u32[]{:S(2)}) %collective-permute-start.3) | collective-permute-done | bytes 1048608 | tf_op jit(solution)/shard_map/ppermute | solution.py:162
  150.5 14.2 %collective-permute-done.4.low_ref = bf16[2,2,1024,128]{3,2,1,0:T(8,128)(2,1)} collective-permute-done((bf16[2,2,1024,128]{3,2,1,0:T(8,128)(2,1)S(1)}, bf16[2,2,1024,128]{3,2,1,0:T(8,128)(2,1)}, u32[]{:S(2)}, u32[]{:S(2)}) %collective-permute-start.4) | collective-permute-done | bytes 1048608 | tf_op jit(solution)/shard_map/ppermute | solution.py:162
  164.7 16.7 %collective-permute-done.5.high_ref = bf16[2,2,1024,128]{3,2,1,0:T(8,128)(2,1)} collective-permute-done((bf16[2,2,1024,128]{3,2,1,0:T(8,128)(2,1)S(1)}, bf16[2,2,1024,128]{3,2,1,0:T(8,128)(2,1)}, u32[]{:S(2)}, u32[]{:S(2)}) %collective-permute-start.5) | collective-permute-done | bytes 1048608 | tf_op jit(solution)/shard_map/ppermute | solution.py:162
  181.4 25.4 %shard_map.96 = (bf16[8,2,256,128]{3,2,1,0:T(8,128)(2,1)}, bf16[8,2,2,256,128]{4,3,2,1,0:T(8,128)(2,1)}, bf16[4,2,2,256,128]{4,3,2,1,0:T(8,128)(2,1)}, bf16[4,2,2,256,128]{4,3,2,1,0:T(8,128)(2,1)}) custom-call(s32[64]{0:T(128)S(1)} %reshape.30.lists, s32[32]{0:T(128)S(1)} %pad_dynamic-slice_fusion.key_counts, s32[16]{0:T(128)S(1)} %dynamic_slice.11.query_counts, ...), custom_call_target="tpu_custom_call" | custom-call | flops 10737418240 | bytes 12582912 | tf_op jit(solution)/shard_map/pallas_call | solution.py:124
  210.7 25.2 %shard_map.95 = (bf16[8,2,256,128]{3,2,1,0:T(8,128)(2,1)}, bf16[8,2,2,256,128]{4,3,2,1,0:T(8,128)(2,1)}, bf16[4,2,2,256,128]{4,3,2,1,0:T(8,128)(2,1)}, bf16[4,2,2,256,128]{4,3,2,1,0:T(8,128)(2,1)}) custom-call(s32[64]{0:T(128)S(1)} %reshape.30.lists, s32[32]{0:T(128)S(1)} %pad_dynamic-slice_fusion.key_counts, s32[16]{0:T(128)S(1)} %dynamic_slice.11.query_counts, ...), custom_call_target="tpu_custom_call" | custom-call | flops 10737418240 | bytes 12582912 | tf_op jit(solution)/shard_map/pallas_call | solution.py:124
  253.0 25.4 %shard_map.94 = (bf16[8,2,256,128]{3,2,1,0:T(8,128)(2,1)}, bf16[8,2,2,256,128]{4,3,2,1,0:T(8,128)(2,1)}, bf16[4,2,2,256,128]{4,3,2,1,0:T(8,128)(2,1)}, bf16[4,2,2,256,128]{4,3,2,1,0:T(8,128)(2,1)}) custom-call(s32[64]{0:T(128)S(1)} %reshape.30.lists, s32[32]{0:T(128)S(1)} %pad_dynamic-slice_fusion.key_counts, s32[16]{0:T(128)S(1)} %dynamic_slice.11.query_counts, ...), custom_call_target="tpu_custom_call" | custom-call | flops 10737418240 | bytes 12582912 | tf_op jit(solution)/shard_map/pallas_call | solution.py:124
  283.5 10.2 %collective-permute-done.7.high_ref = bf16[2,2,1024,128]{3,2,1,0:T(8,128)(2,1)} collective-permute-done((bf16[2,2,1024,128]{3,2,1,0:T(8,128)(2,1)}, bf16[2,2,1024,128]{3,2,1,0:T(8,128)(2,1)}, u32[]{:S(2)}, u32[]{:S(2)}) %collective-permute-start.7) | collective-permute-done | bytes 1048608 | tf_op jit(solution)/shard_map/ppermute | solution.py:162
  293.8 25.2 %shard_map.97 = (bf16[8,2,256,128]{3,2,1,0:T(8,128)(2,1)}, bf16[8,2,2,256,128]{4,3,2,1,0:T(8,128)(2,1)}, bf16[4,2,2,256,128]{4,3,2,1,0:T(8,128)(2,1)}, bf16[4,2,2,256,128]{4,3,2,1,0:T(8,128)(2,1)}) custom-call(s32[64]{0:T(128)S(1)} %reshape.30.lists, s32[32]{0:T(128)S(1)} %pad_dynamic-slice_fusion.key_counts, s32[16]{0:T(128)S(1)} %dynamic_slice.11.query_counts, ...), custom_call_target="tpu_custom_call" | custom-call | flops 10737418240 | bytes 12582912 | tf_op jit(solution)/shard_map/pallas_call | solution.py:124
  331.1 22.3 %collective-permute-done.8 = bf16[4,2,2,256,128]{4,3,2,1,0:T(8,128)(2,1)S(1)} collective-permute-done((bf16[4,2,2,256,128]{4,3,2,1,0:T(8,128)(2,1)}, bf16[4,2,2,256,128]{4,3,2,1,0:T(8,128)(2,1)S(1)}, u32[]{:S(2)}, u32[]{:S(2)}) %collective-permute-start.8) | collective-permute-done | bytes 1048608 | tf_op jit(solution)/shard_map/ppermute | solution.py:162
  353.4 18.5 %collective-permute-done.9 = bf16[4,2,2,256,128]{4,3,2,1,0:T(8,128)(2,1)S(1)} collective-permute-done((bf16[4,2,2,256,128]{4,3,2,1,0:T(8,128)(2,1)}, bf16[4,2,2,256,128]{4,3,2,1,0:T(8,128)(2,1)S(1)}, u32[]{:S(2)}, u32[]{:S(2)}) %collective-permute-start.9) | collective-permute-done | bytes 1048608 | tf_op jit(solution)/shard_map/ppermute | solution.py:162
  388.6 22.3 %collective-permute-done.10 = bf16[4,2,2,256,128]{4,3,2,1,0:T(8,128)(2,1)S(1)} collective-permute-done((bf16[4,2,2,256,128]{4,3,2,1,0:T(8,128)(2,1)}, bf16[4,2,2,256,128]{4,3,2,1,0:T(8,128)(2,1)S(1)}, u32[]{:S(2)}, u32[]{:S(2)}) %collective-permute-start.10) | collective-permute-done | bytes 1048608 | tf_op jit(solution)/shard_map/ppermute | solution.py:162
  410.9 18.5 %collective-permute-done.11 = bf16[4,2,2,256,128]{4,3,2,1,0:T(8,128)(2,1)S(1)} collective-permute-done((bf16[4,2,2,256,128]{4,3,2,1,0:T(8,128)(2,1)}, bf16[4,2,2,256,128]{4,3,2,1,0:T(8,128)(2,1)S(1)}, u32[]{:S(2)}, u32[]{:S(2)}) %collective-permute-start.11) | collective-permute-done | bytes 1048608 | tf_op jit(solution)/shard_map/ppermute | solution.py:162
  456.0 11.6 %collective-permute-done.12 = bf16[4,2,2,256,128]{4,3,2,1,0:T(8,128)(2,1)} collective-permute-done((bf16[4,2,2,256,128]{4,3,2,1,0:T(8,128)(2,1)}, bf16[4,2,2,256,128]{4,3,2,1,0:T(8,128)(2,1)}, u32[]{:S(2)}, u32[]{:S(2)}) %collective-permute-start.12) | collective-permute-done | bytes 1048608 | tf_op jit(solution)/shard_map/ppermute | solution.py:162
  467.6 18.4 %collective-permute-done.13 = bf16[4,2,2,256,128]{4,3,2,1,0:T(8,128)(2,1)} collective-permute-done((bf16[4,2,2,256,128]{4,3,2,1,0:T(8,128)(2,1)}, bf16[4,2,2,256,128]{4,3,2,1,0:T(8,128)(2,1)}, u32[]{:S(2)}, u32[]{:S(2)}) %collective-permute-start.13) | collective-permute-done | bytes 1048608 | tf_op jit(solution)/shard_map/ppermute | solution.py:162
  497.9 21.8 %collective-permute-done.14 = bf16[4,2,2,256,128]{4,3,2,1,0:T(8,128)(2,1)S(1)} collective-permute-done((bf16[4,2,2,256,128]{4,3,2,1,0:T(8,128)(2,1)S(1)}, bf16[4,2,2,256,128]{4,3,2,1,0:T(8,128)(2,1)S(1)}, u32[]{:S(2)}, u32[]{:S(2)}) %collective-permute-start.14) | collective-permute-done | bytes 1048608 | tf_op jit(solution)/shard_map/ppermute | solution.py:162
  519.7 17.8 %collective-permute-done.15 = bf16[4,2,2,256,128]{4,3,2,1,0:T(8,128)(2,1)S(1)} collective-permute-done((bf16[4,2,2,256,128]{4,3,2,1,0:T(8,128)(2,1)S(1)}, bf16[4,2,2,256,128]{4,3,2,1,0:T(8,128)(2,1)S(1)}, u32[]{:S(2)}, u32[]{:S(2)}) %collective-permute-start.15) | collective-permute-done | bytes 1048608 | tf_op jit(solution)/shard_map/ppermute | solution.py:162
  539.7 30.9 %all_to_all.50 = bf16[8,2,256,128]{3,2,1,0:T(8,128)(2,1)} all-to-all(bf16[8,2,256,128]{3,2,1,0:T(8,128)(2,1)S(1)} %get-tuple-element.100), channel_id=1, replica_groups=mesh['seq'=4,'head'=8] {'head'}, dimensions={0} | all-to-all | bytes 2097152 | tf_op jit(solution)/shard_map/all_to_all | solution.py:166
  575.0 49.1 %all-to-all-done.7 = bf16[8,2,2,256,128]{4,3,2,1,0:T(8,128)(2,1)} async-done(((bf16[8,2,2,256,128]{4,3,2,1,0:T(8,128)(2,1)}), bf16[8,2,2,256,128]{4,3,2,1,0:T(8,128)(2,1)}, u32[]{:S(2)}, u32[]{:S(2)}) %all-to-all-start.7) | async-done | bytes 2097184 | tf_op jit(solution)/shard_map/all_to_all | solution.py:166
  627.6 7.8 %copy.146 = bf16[256,4,2048]{2,1,0:T(4,128)(2,1)} copy(bf16[256,4,2048]{0,2,1:T(8,128)(2,1)} %bitcast.107) | data formatting | bytes 8388608
  650.3 7.9 %copy.147 = bf16[256,4,2048]{2,1,0:T(4,128)(2,1)} copy(bf16[256,4,2048]{0,2,1:T(8,128)(2,1)} %bitcast.110) | data formatting | bytes 8388608
  (116 shorter events, 192.7 us)
Async XLA Ops:
  32.0 149.4 %all-to-all-start = ((bf16[8,8,256,128]{3,2,1,0:T(8,128)(2,1)}), bf16[8,8,256,128]{3,2,1,0:T(8,128)(2,1)}, u32[]{:S(2)}, u32[]{:S(2)}) async-start(bf16[8,8,256,128]{3,2,1,0:T(8,128)(2,1)} %bitcast.106), calls=%async_computation | async-start | bytes 8388608 | tf_op jit(solution)/shard_map/all_to_all | solution.py:166
  40.3 46.7 %collective-permute-start = (bf16[2,2,1024,128]{3,2,1,0:T(8,128)(2,1)}, bf16[2,2,1024,128]{3,2,1,0:T(8,128)(2,1)S(1)}, u32[]{:S(2)}, u32[]{:S(2)}) collective-permute-start(bf16[2,2,1024,128]{3,2,1,0:T(8,128)(2,1)} %pad_maximum_fusion.4.own_high_ref), channel_id=1, source_target_pairs={{0,8},{8,16},{16,24},{1,9},{9,17},{17,25},{2,10},{10,18},{18,26},{... | collective-permute-start | bytes 3145736 | tf_op jit(solution)/shard_map/ppermute | solution.py:162
  87.0 28.8 %collective-permute-start.2 = (bf16[2,2,1024,128]{3,2,1,0:T(8,128)(2,1)S(1)}, bf16[2,2,1024,128]{3,2,1,0:T(8,128)(2,1)S(1)}, u32[]{:S(2)}, u32[]{:S(2)}) collective-permute-start(bf16[2,2,1024,128]{3,2,1,0:T(8,128)(2,1)S(1)} %pad_maximum_fusion.6.own_high_ref), channel_id=1, source_target_pairs={{0,8},{8,16},{16,24},{1,9},{9,17},{17,25},{2,10},{10,18},{18,26},{... | collective-permute-start | bytes 3145736 | tf_op jit(solution)/shard_map/ppermute | solution.py:162
  90.4 44.9 %collective-permute-start.3 = (bf16[2,2,1024,128]{3,2,1,0:T(8,128)(2,1)S(1)}, bf16[2,2,1024,128]{3,2,1,0:T(8,128)(2,1)S(1)}, u32[]{:S(2)}, u32[]{:S(2)}) collective-permute-start(bf16[2,2,1024,128]{3,2,1,0:T(8,128)(2,1)S(1)} %pad_maximum_fusion.5.own_low_ref), channel_id=1, source_target_pairs={{8,0},{16,8},{24,16},{9,1},{17,9},{25,17},{10,2},{18,10},{26,18},{... | collective-permute-start | bytes 3145736 | tf_op jit(solution)/shard_map/ppermute | solution.py:162
  135.3 29.5 %collective-permute-start.4 = (bf16[2,2,1024,128]{3,2,1,0:T(8,128)(2,1)S(1)}, bf16[2,2,1024,128]{3,2,1,0:T(8,128)(2,1)}, u32[]{:S(2)}, u32[]{:S(2)}) collective-permute-start(bf16[2,2,1024,128]{3,2,1,0:T(8,128)(2,1)S(1)} %pad_maximum_fusion.8.own_high_ref), channel_id=1, source_target_pairs={{0,8},{8,16},{16,24},{1,9},{9,17},{17,25},{2,10},{10,18},{18,26},{... | collective-permute-start | bytes 3145736 | tf_op jit(solution)/shard_map/ppermute | solution.py:162
  137.2 44.3 %collective-permute-start.5 = (bf16[2,2,1024,128]{3,2,1,0:T(8,128)(2,1)S(1)}, bf16[2,2,1024,128]{3,2,1,0:T(8,128)(2,1)}, u32[]{:S(2)}, u32[]{:S(2)}) collective-permute-start(bf16[2,2,1024,128]{3,2,1,0:T(8,128)(2,1)S(1)} %pad_maximum_fusion.7.own_low_ref), channel_id=1, source_target_pairs={{8,0},{16,8},{24,16},{9,1},{17,9},{25,17},{10,2},{18,10},{26,18},{... | collective-permute-start | bytes 3145736 | tf_op jit(solution)/shard_map/ppermute | solution.py:162
  206.8 30.5 %all-to-all-start.3 = ((bf16[8,2,256,128]{3,2,1,0:T(8,128)(2,1)}), bf16[8,2,256,128]{3,2,1,0:T(8,128)(2,1)S(1)}, u32[]{:S(2)}, u32[]{:S(2)}) async-start(bf16[8,2,256,128]{3,2,1,0:T(8,128)(2,1)} %get-tuple-element.46), calls=%async_computation.3 | async-start | bytes 2097152 | tf_op jit(solution)/shard_map/all_to_all | solution.py:166
  237.3 41.1 %all-to-all-start.2 = ((bf16[8,2,256,128]{3,2,1,0:T(8,128)(2,1)}), bf16[8,2,256,128]{3,2,1,0:T(8,128)(2,1)S(1)}, u32[]{:S(2)}, u32[]{:S(2)}) async-start(bf16[8,2,256,128]{3,2,1,0:T(8,128)(2,1)} %get-tuple-element.43), calls=%async_computation.2 | async-start | bytes 2097152 | tf_op jit(solution)/shard_map/all_to_all | solution.py:166
  245.7 37.8 %collective-permute-start.6 = (bf16[2,2,1024,128]{3,2,1,0:T(8,128)(2,1)}, bf16[2,2,1024,128]{3,2,1,0:T(8,128)(2,1)}, u32[]{:S(2)}, u32[]{:S(2)}) collective-permute-start(bf16[2,2,1024,128]{3,2,1,0:T(8,128)(2,1)} %pad_maximum_fusion.10.own_high_ref), channel_id=1, source_target_pairs={{0,8},{8,16},{16,24},{1,9},{9,17},{17,25},{2,10},{10,18},{18,26},{... | collective-permute-start | bytes 3145736 | tf_op jit(solution)/shard_map/ppermute | solution.py:162
  247.6 46.1 %collective-permute-start.7 = (bf16[2,2,1024,128]{3,2,1,0:T(8,128)(2,1)}, bf16[2,2,1024,128]{3,2,1,0:T(8,128)(2,1)}, u32[]{:S(2)}, u32[]{:S(2)}) collective-permute-start(bf16[2,2,1024,128]{3,2,1,0:T(8,128)(2,1)} %pad_maximum_fusion.9.own_low_ref), channel_id=1, source_target_pairs={{8,0},{16,8},{24,16},{9,1},{17,9},{25,17},{10,2},{18,10},{26,18},{... | collective-permute-start | bytes 3145736 | tf_op jit(solution)/shard_map/ppermute | solution.py:162
  278.4 40.6 %all-to-all-start.1 = ((bf16[8,2,256,128]{3,2,1,0:T(8,128)(2,1)}), bf16[8,2,256,128]{3,2,1,0:T(8,128)(2,1)}, u32[]{:S(2)}, u32[]{:S(2)}) async-start(bf16[8,2,256,128]{3,2,1,0:T(8,128)(2,1)} %get-tuple-element.40), calls=%async_computation.1 | async-start | bytes 2097152 | tf_op jit(solution)/shard_map/all_to_all | solution.py:166
  319.0 56.6 %all-to-all-start.4 = ((bf16[8,2,256,128]{3,2,1,0:T(8,128)(2,1)}), bf16[8,2,256,128]{3,2,1,0:T(8,128)(2,1)S(1)}, u32[]{:S(2)}, u32[]{:S(2)}) async-start(bf16[8,2,256,128]{3,2,1,0:T(8,128)(2,1)} %get-tuple-element.49), calls=%async_computation.4 | async-start | bytes 2097152 | tf_op jit(solution)/shard_map/all_to_all | solution.py:166
  323.8 29.6 %collective-permute-start.8 = (bf16[4,2,2,256,128]{4,3,2,1,0:T(8,128)(2,1)}, bf16[4,2,2,256,128]{4,3,2,1,0:T(8,128)(2,1)S(1)}, u32[]{:S(2)}, u32[]{:S(2)}) collective-permute-start(bf16[4,2,2,256,128]{4,3,2,1,0:T(8,128)(2,1)} %get-tuple-element.53), channel_id=1, source_target_pairs={{0,8},{8,16},{16,24},{1,9},{9,17},{17,25},{2,10},{10,18},{18,26},{... | collective-permute-start | bytes 3145736 | tf_op jit(solution)/shard_map/ppermute | solution.py:162
  325.7 46.1 %collective-permute-start.9 = (bf16[4,2,2,256,128]{4,3,2,1,0:T(8,128)(2,1)}, bf16[4,2,2,256,128]{4,3,2,1,0:T(8,128)(2,1)S(1)}, u32[]{:S(2)}, u32[]{:S(2)}) collective-permute-start(bf16[4,2,2,256,128]{4,3,2,1,0:T(8,128)(2,1)} %get-tuple-element.54), channel_id=1, source_target_pairs={{8,0},{16,8},{24,16},{9,1},{17,9},{25,17},{10,2},{18,10},{26,18},{... | collective-permute-start | bytes 3145736 | tf_op jit(solution)/shard_map/ppermute | solution.py:162
  376.5 56.6 %all-to-all-start.5 = ((bf16[8,2,2,256,128]{4,3,2,1,0:T(8,128)(2,1)}), bf16[8,2,2,256,128]{4,3,2,1,0:T(8,128)(2,1)S(1)}, u32[]{:S(2)}, u32[]{:S(2)}) async-start(bf16[8,2,2,256,128]{4,3,2,1,0:T(8,128)(2,1)} %add_convert_fusion.3), calls=%async_computation.5 | async-start | bytes 4194304 | tf_op jit(solution)/shard_map/all_to_all | solution.py:166
  381.3 29.6 %collective-permute-start.10 = (bf16[4,2,2,256,128]{4,3,2,1,0:T(8,128)(2,1)}, bf16[4,2,2,256,128]{4,3,2,1,0:T(8,128)(2,1)S(1)}, u32[]{:S(2)}, u32[]{:S(2)}) collective-permute-start(bf16[4,2,2,256,128]{4,3,2,1,0:T(8,128)(2,1)} %get-tuple-element.58), channel_id=1, source_target_pairs={{0,8},{8,16},{16,24},{1,9},{9,17},{17,25},{2,10},{10,18},{18,26},{... | collective-permute-start | bytes 3145736 | tf_op jit(solution)/shard_map/ppermute | solution.py:162
  383.2 46.1 %collective-permute-start.11 = (bf16[4,2,2,256,128]{4,3,2,1,0:T(8,128)(2,1)}, bf16[4,2,2,256,128]{4,3,2,1,0:T(8,128)(2,1)S(1)}, u32[]{:S(2)}, u32[]{:S(2)}) collective-permute-start(bf16[4,2,2,256,128]{4,3,2,1,0:T(8,128)(2,1)} %get-tuple-element.59), channel_id=1, source_target_pairs={{8,0},{16,8},{24,16},{9,1},{17,9},{25,17},{10,2},{18,10},{26,18},{... | collective-permute-start | bytes 3145736 | tf_op jit(solution)/shard_map/ppermute | solution.py:162
  433.2 106.5 %all-to-all-start.6 = ((bf16[8,2,2,256,128]{4,3,2,1,0:T(8,128)(2,1)}), bf16[8,2,2,256,128]{4,3,2,1,0:T(8,128)(2,1)}, u32[]{:S(2)}, u32[]{:S(2)}) async-start(bf16[8,2,2,256,128]{4,3,2,1,0:T(8,128)(2,1)} %add_convert_fusion.2), calls=%async_computation.6 | async-start | bytes 4194304 | tf_op jit(solution)/shard_map/all_to_all | solution.py:166
  437.9 29.7 %collective-permute-start.12 = (bf16[4,2,2,256,128]{4,3,2,1,0:T(8,128)(2,1)}, bf16[4,2,2,256,128]{4,3,2,1,0:T(8,128)(2,1)}, u32[]{:S(2)}, u32[]{:S(2)}) collective-permute-start(bf16[4,2,2,256,128]{4,3,2,1,0:T(8,128)(2,1)} %get-tuple-element.63), channel_id=1, source_target_pairs={{0,8},{8,16},{16,24},{1,9},{9,17},{17,25},{2,10},{10,18},{18,26},{... | collective-permute-start | bytes 3145736 | tf_op jit(solution)/shard_map/ppermute | solution.py:162
  439.8 46.1 %collective-permute-start.13 = (bf16[4,2,2,256,128]{4,3,2,1,0:T(8,128)(2,1)}, bf16[4,2,2,256,128]{4,3,2,1,0:T(8,128)(2,1)}, u32[]{:S(2)}, u32[]{:S(2)}) collective-permute-start(bf16[4,2,2,256,128]{4,3,2,1,0:T(8,128)(2,1)} %get-tuple-element.64), channel_id=1, source_target_pairs={{8,0},{16,8},{24,16},{9,1},{17,9},{25,17},{10,2},{18,10},{26,18},{... | collective-permute-start | bytes 3145736 | tf_op jit(solution)/shard_map/ppermute | solution.py:162
  490.4 29.3 %collective-permute-start.14 = (bf16[4,2,2,256,128]{4,3,2,1,0:T(8,128)(2,1)S(1)}, bf16[4,2,2,256,128]{4,3,2,1,0:T(8,128)(2,1)S(1)}, u32[]{:S(2)}, u32[]{:S(2)}) collective-permute-start(bf16[4,2,2,256,128]{4,3,2,1,0:T(8,128)(2,1)S(1)} %copy-done.15), channel_id=1, source_target_pairs={{0,8},{8,16},{16,24},{1,9},{9,17},{17,25},{2,10},{10,18},{18,26},{... | collective-permute-start | bytes 3145736 | tf_op jit(solution)/shard_map/ppermute | solution.py:162
  492.5 45.0 %collective-permute-start.15 = (bf16[4,2,2,256,128]{4,3,2,1,0:T(8,128)(2,1)S(1)}, bf16[4,2,2,256,128]{4,3,2,1,0:T(8,128)(2,1)S(1)}, u32[]{:S(2)}, u32[]{:S(2)}) collective-permute-start(bf16[4,2,2,256,128]{4,3,2,1,0:T(8,128)(2,1)S(1)} %copy-done.14), channel_id=1, source_target_pairs={{8,0},{16,8},{24,16},{9,1},{17,9},{25,17},{10,2},{18,10},{26,18},{... | collective-permute-start | bytes 3145736 | tf_op jit(solution)/shard_map/ppermute | solution.py:162
  570.6 53.4 %all-to-all-start.7 = ((bf16[8,2,2,256,128]{4,3,2,1,0:T(8,128)(2,1)}), bf16[8,2,2,256,128]{4,3,2,1,0:T(8,128)(2,1)}, u32[]{:S(2)}, u32[]{:S(2)}) async-start(bf16[8,2,2,256,128]{4,3,2,1,0:T(8,128)(2,1)} %add_convert_fusion.1), calls=%async_computation.7 | async-start | bytes 4194304 | tf_op jit(solution)/shard_map/all_to_all | solution.py:166
  624.0 34.2 %all-to-all-start.9 = ((bf16[8,2,256,128]{3,2,1,0:T(8,128)(2,1)}), bf16[8,2,256,128]{3,2,1,0:T(8,128)(2,1)S(1)}, u32[]{:S(2)}, u32[]{:S(2)}) async-start(bf16[8,2,256,128]{3,2,1,0:T(8,128)(2,1)} %get-tuple-element.70), calls=%async_computation.9 | async-start | bytes 2097152 | tf_op jit(solution)/shard_map/all_to_all | solution.py:166
  (20 other events, 610.6 us)
